TPU v7x, 32 devices: a whole 2x2x4 slice. The times are simulated.
32 devices in a mesh: section: 2 (over x), hid: 4 (over z), wid: 4 (over y, core).
Axes of the slice: x: 2, y: 2, z: 4, core: 2. Of those that a mesh axis runs over, the one named last changes fastest.
Arguments:
- grad_out: float32 [2, 256, 6144], P(None, None, 'wid'), may hold values from -6 to 6
- weight_in: bfloat16 [2, 6144, 24576], P('section', 'wid', 'hid'), may hold values from -0.078125 to 0.078125
- weight_out: bfloat16 [2, 24576, 6144], P('section', 'hid', 'wid'), may hold values from -0.0390625 to 0.0390625
- pre_act: float32 [2, 2, 256, 24576], P('section', None, None, 'hid'), may hold values from -6 to 6
Outputs:
- grads: float32 [2, 2, 256, 6144], P('section', None, None, 'wid')
All inputs are finite; a program needn't handle non-finite values.
Results may differ from a plain program's by a relative error of at most 0.003.
Values may be sent and summed in bfloat16 or wider, within the bound.
No kernel may reach another device: no remote copies, remote signals or barrier semaphores. Data moves between devices by JAX's collectives and lax.ppermute only.
A program may use at most 192 MiB of HBM per device.

v0:
```python
import jax
import jax.numpy as jnp
from jax import lax
from jax.sharding import PartitionSpec as P


def swapped(shard, axis, distance):
    return lax.ppermute(shard, axis, [(i, i ^ 1 << distance) for i in range(lax.axis_size(axis))])


def from_behind(block, axis, distance):
    devices = range(lax.axis_size(axis))
    route = [(i - distance, i) for i in devices if i - distance in devices]
    return lax.ppermute(block, axis, route)


def gelu_slope(pre):
    normal_cdf = 0.5 * (1.0 + jax.scipy.special.erf(pre * 0.7071067811865476))
    density = jnp.exp(-0.5 * pre * pre) * 0.3989422804014327
    return normal_cdf + pre * density


def local(grad_out, weight_in, weight_out, pre_act):
    section_pos = lax.axis_index("section")
    wid_pos = lax.axis_index("wid")
    is_down = section_pos == 0
    low_side = wid_pos % 2 == 0
    tile_in = weight_in[0]
    tile_out = weight_out[0]
    saved_pre = pre_act[0]
    quarter = tile_in.shape[0]
    hid_tile = tile_in.shape[1]
    half_tile = hid_tile // 2
    out_view = tile_out.reshape(half_tile, 2 * quarter)
    out_low = jnp.where(is_down, tile_out[:half_tile], out_view[:, :quarter])
    out_high = jnp.where(is_down, tile_out[half_tile:], out_view[:, quarter:])
    in_view = tile_in.reshape(2 * quarter, half_tile)
    in_low = jnp.where(is_down, tile_in[:, :half_tile], in_view[:quarter])
    in_high = jnp.where(is_down, tile_in[:, half_tile:], in_view[quarter:])
    batches = grad_out.shape[0]
    contract = (((1,), (1,)), ((), ()))
    results = []
    received = None
    for moment in range(batches + 1):
        fresh_grad = grad_out[min(moment, batches - 1)]
        batch_pick = jnp.clip(moment - section_pos, 0, batches - 1)
        pre_now = lax.dynamic_index_in_dim(saved_pre, batch_pick, 0, keepdims=False)
        if received is None:
            arrived = jnp.zeros_like(fresh_grad)
            partner = jnp.zeros(fresh_grad.shape, jnp.bfloat16)
        else:
            arrived = received
            partner = swapped(arrived.astype(jnp.bfloat16), "wid", 0)
        own_in = jnp.where(is_down, fresh_grad, arrived)
        fresh_low = fresh_grad.astype(jnp.bfloat16)
        arrived_low = arrived.astype(jnp.bfloat16)
        first_in = jnp.where(is_down, fresh_low, jnp.where(low_side, arrived_low, partner))
        second_in = jnp.where(is_down, fresh_low, jnp.where(low_side, partner, arrived_low))
        low_hidden = lax.dot_general(
            first_in, out_low, contract, preferred_element_type=jnp.float32
        )
        high_hidden = lax.dot_general(
            second_in, out_high, contract, preferred_element_type=jnp.float32
        )
        joined = low_hidden + high_hidden
        empty_slot = jnp.zeros_like(joined)
        up_part = jnp.concatenate(
            [jnp.where(low_side, joined, empty_slot), jnp.where(low_side, empty_slot, joined)],
            axis=1,
        )
        partial_hidden = jnp.where(
            is_down, jnp.concatenate([low_hidden, high_hidden], axis=1), up_part
        )
        hidden_grad = lax.psum(partial_hidden, "wid")
        hidden = (hidden_grad * gelu_slope(pre_now)).astype(jnp.bfloat16)
        own_slot = jnp.where(low_side, hidden[:, :half_tile], hidden[:, half_tile:])
        first_hidden = jnp.where(is_down, hidden[:, :half_tile], own_slot)
        second_hidden = jnp.where(is_down, hidden[:, half_tile:], own_slot)
        low_term = lax.dot_general(
            first_hidden, in_low, contract, preferred_element_type=jnp.float32
        )
        high_term = lax.dot_general(
            second_hidden, in_high, contract, preferred_element_type=jnp.float32
        )
        own_term = jnp.where(
            is_down, low_term + high_term, jnp.where(low_side, low_term, high_term)
        )
        send_term = jnp.where(
            is_down, jnp.zeros_like(low_term), jnp.where(low_side, high_term, low_term)
        )
        own_term, send_term = (own_term, send_term)
        partial_value = own_term + swapped(send_term, "wid", 0)
        result = own_in + lax.psum(partial_value, "hid")
        results.append(result)
        if moment < batches:
            received = from_behind(result, "section", 1)
    chosen = jnp.stack(
        [jnp.where(is_down, results[index_m], results[index_m + 1]) for index_m in range(batches)]
    )
    return chosen[None]


def solution(mesh):
    return jax.shard_map(
        local,
        mesh=mesh,
        in_specs=(
            P(None, None, "wid"),
            P("section", "wid", "hid"),
            P("section", "hid", "wid"),
            P("section", None, None, "hid"),
        ),
        out_specs=P("section", None, None, "wid"),
        check_vma=False,
    )
```

profile of v0, /device:TPU:2, one launch (start us, length us, event | category | flops | bytes accessed | tf_op | source)
XLA Modules:
  0.0 849.3 jit_solution(3926321926453295962)
XLA Ops:
  6.5 27.3 %reshape_squeeze.4 = bf16[3072,3072]{1,0:T(8,128)(2,1)} reshape(bf16[1,6144,1536]{2,1,0:T(8,128)(2,1)} %param.6) | data formatting | bytes 37748736 | tf_op jit(solution)/shard_map/reshape;squeeze | solution.py:34
  33.9 12.6 %slice_select_fusion.3 = (bf16[3072,1536]{1,0:T(8,128)(2,1)S(1)}, bf16[3072,1536]{1,0:T(8,128)(2,1)S(1)}) fusion(bf16[3072,3072]{1,0:T(8,128)(2,1)} %reshape_squeeze.4, bf16[1,6144,1536]{2,1,0:T(8,128)(2,1)} %param.6, pred[]{:T(512)S(6)} %eq.8), kind=kLoop, calls=%fused_computation.6 | loop fusion | flops 9437184 | bytes 56623104 | tf_op jit(solution)/shard_map/jit(_where)/select_n | solution.py:35
  61.1 7.8 maximum_select_fusion
  69.0 14.3 %fusion.90 = (bf16[1,768,6144]{2,1,0:T(8,128)(2,1)}, bf16[1,768,6144]{2,1,0:T(8,128)(2,1)}) fusion(bf16[1,1536,6144]{2,1,0:T(8,128)(2,1)} %param.5), kind=kLoop, calls=%fused_computation.125 | loop fusion | bytes 37748736 | tf_op jit(solution)/shard_map/slice | solution.py:38
  83.3 13.7 %slice.78 = bf16[1536,3072]{1,0:T(8,128)(2,1)} reshape(bf16[1,768,6144]{2,1,0:T(8,128)(2,1)} %get-tuple-element.11) | data formatting | bytes 18874368 | tf_op jit(solution)/shard_map/slice | solution.py:38
  96.9 13.7 %slice.81 = bf16[1536,3072]{1,0:T(8,128)(2,1)} reshape(bf16[1,768,6144]{2,1,0:T(8,128)(2,1)} %get-tuple-element.12) | data formatting | bytes 18874368 | tf_op jit(solution)/shard_map/slice | solution.py:39
  110.7 20.0 %slice_select_fusion.1 = (bf16[1536,3072]{1,0:T(8,128)(2,1)}, bf16[1536,3072]{1,0:T(8,128)(2,1)}) fusion(bf16[1536,3072]{1,0:T(8,128)(2,1)} %slice.78, bf16[1536,6144]{1,0:T(8,128)(2,1)} %bitcast.93, pred[]{:T(512)S(6)} %eq.8, bf16[1536,3072]{1,0:T(8,128)(2,1)} %slice.81), kind=kLoop, calls=%fused_computation.4 | loop fusion | flops 9437184 | bytes 56623104 | tf_op jit(solution)/shard_map/jit(_where)/select_n | solution.py:38
  130.7 59.2 %all-reduce.7.cloned.1.call-done = f32[256,6144]{1,0:T(8,128)} async-done(((f32[256,6144]{1,0:T(8,128)}), f32[256,6144]{1,0:T(8,128)}) %all-reduce.7.cloned.1.call-update) | async-done | bytes 6291472 | tf_op jit(solution)/shard_map/psum | solution.py:74
  189.9 7.2 fusion.5
  211.7 69.4 %all-reduce.9.cloned.1.call-done = f32[256,1536]{1,0:T(8,128)} async-done(((f32[256,1536]{1,0:T(8,128)}), f32[256,1536]{1,0:T(8,128)}) %all-reduce.9.cloned.1.call-update) | async-done | bytes 1572880 | tf_op jit(solution)/shard_map/psum | solution.py:93
  285.6 35.4 %collective-permute-done.1 = f32[256,1536]{1,0:T(8,128)S(1)} collective-permute-done((f32[256,1536]{1,0:T(8,128)S(1)}, f32[256,1536]{1,0:T(8,128)S(1)}, u32[]{:S(2)}, u32[]{:S(2)}) %collective-permute-start.1) | collective-permute-done | bytes 1572896 | tf_op jit(solution)/shard_map/ppermute | solution.py:14
  324.6 8.5 %fusion.69 = f32[256,3072]{1,0:T(8,128)} fusion(bf16[3072,1536]{1,0:T(8,128)(2,1)} %copy-done.3, bf16[256,1536]{1,0:T(8,128)(2,1)S(1)} %collective-permute-done.2, bf16[256,1536]{1,0:T(8,128)(2,1)S(1)} %convert_element_type.30, pred[]{:T(512)S(6)} %eq.9, pred[]{:T(512)S(6)} %eq.8, f32[2,256,1536]{2,1,0:T(8,128)} %param.4), kind=kOutput, calls=%fused_computation.107 | convolution fusion | flops 2416705536 | bytes 14942210 | tf_op jit(solution)/shard_map/dot_general | solution.py:62
  333.2 7.3 broadcast_select_fusion.3
  340.5 7.8 maximum_select_fusion.1
  348.4 120.0 %all-reduce.11.cloned.1.call-done = f32[256,6144]{1,0:T(8,128)} async-done(((f32[256,6144]{1,0:T(8,128)}), f32[256,6144]{1,0:T(8,128)}) %all-reduce.11.cloned.1.call-update) | async-done | bytes 6291472 | tf_op jit(solution)/shard_map/psum | solution.py:74
  468.4 7.2 fusion.11
  488.9 69.4 %all-reduce.13.cloned.1.call-done = f32[256,1536]{1,0:T(8,128)} async-done(((f32[256,1536]{1,0:T(8,128)}), f32[256,1536]{1,0:T(8,128)}) %all-reduce.13.cloned.1.call-update) | async-done | bytes 1572880 | tf_op jit(solution)/shard_map/psum | solution.py:93
  565.3 35.4 %collective-permute-done.4 = f32[256,1536]{1,0:T(8,128)S(1)} collective-permute-done((f32[256,1536]{1,0:T(8,128)S(1)}, f32[256,1536]{1,0:T(8,128)S(1)}, u32[]{:S(2)}, u32[]{:S(2)}) %collective-permute-start.4) | collective-permute-done | bytes 1572896 | tf_op jit(solution)/shard_map/ppermute | solution.py:14
  604.3 8.5 %fusion.63 = f32[256,3072]{1,0:T(8,128)} fusion(bf16[3072,1536]{1,0:T(8,128)(2,1)} %copy-done.3, bf16[256,1536]{1,0:T(8,128)(2,1)S(1)} %collective-permute-done.5, bf16[256,1536]{1,0:T(8,128)(2,1)S(1)} %convert_element_type.32, pred[]{:T(512)S(6)} %eq.9, pred[]{:T(512)S(6)} %eq.8, f32[2,256,1536]{2,1,0:T(8,128)} %param.4), kind=kOutput, calls=%fused_computation.101 | convolution fusion | flops 2416705536 | bytes 14942210 | tf_op jit(solution)/shard_map/dot_general | solution.py:62
  612.9 7.4 broadcast_select_fusion.1
  620.2 7.8 maximum_select_fusion.2
  628.1 120.0 %all-reduce.15.cloned.1.call-done = f32[256,6144]{1,0:T(8,128)} async-done(((f32[256,6144]{1,0:T(8,128)}), f32[256,6144]{1,0:T(8,128)}) %all-reduce.15.cloned.1.call-update) | async-done | bytes 6291472 | tf_op jit(solution)/shard_map/psum | solution.py:74
  748.1 7.2 fusion.17
  768.5 69.5 %all-reduce.17.cloned.1.call-done = f32[256,1536]{1,0:T(8,128)} async-done(((f32[256,1536]{1,0:T(8,128)}), f32[256,1536]{1,0:T(8,128)}) %all-reduce.17.cloned.1.call-update) | async-done | bytes 1572880 | tf_op jit(solution)/shard_map/psum | solution.py:93
  (96 shorter events, 78.7 us)
Async XLA Ops:
  6.5 183.4 %all-reduce.7.cloned.1.call-start = ((), (), s32[]{:S(2)}) async-start(), calls=%async_computation | async-start | bytes 12582912 | tf_op jit(solution)/shard_map/psum | solution.py:74
  33.9 16.2 %copy-start.1 = (f32[2,256,1536]{2,1,0:T(8,128)S(1)}, f32[2,256,1536]{2,1,0:T(8,128)}, u32[]{:S(2)}) copy-start(f32[2,256,1536]{2,1,0:T(8,128)} %param.4) | copy-start | bytes 9437188
  69.0 212.2 %all-reduce.9.cloned.1.call-start = ((), (), s32[]{:S(2)}) async-start(), calls=%async_computation.1 | async-start | bytes 3145728 | tf_op jit(solution)/shard_map/psum | solution.py:93
  189.9 12.7 %slice-start.7 = ((s8[9437184]{0:T(1024)(128)(4,1)}), s8[4194304]{0:T(1024)(128)(4,1)S(1)}, s32[]{:S(2)}) async-start(s8[9437184]{0:T(1024)(128)(4,1)} %bitcast.94), calls=%async_computation.13 | async-start | bytes 8388608
  206.4 3.6 collective-permute-start
  211.7 256.7 %all-reduce.11.cloned.1.call-start = ((), (), s32[]{:S(2)}) async-start(), calls=%async_computation.2 | async-start | bytes 12582912 | tf_op jit(solution)/shard_map/psum | solution.py:74
  281.1 52.0 %slice-start = ((s8[9437184]{0:T(1024)(128)(4,1)}), s8[4194304]{0:T(1024)(128)(4,1)S(1)}, s32[]{:S(2)}) async-start(s8[9437184]{0:T(1024)(128)(4,1)} %bitcast.89), calls=%async_computation.6 | async-start | bytes 8388608
  284.1 36.9 %collective-permute-start.1 = (f32[256,1536]{1,0:T(8,128)S(1)}, f32[256,1536]{1,0:T(8,128)S(1)}, u32[]{:S(2)}, u32[]{:S(2)}) collective-permute-start(f32[256,1536]{1,0:T(8,128)S(1)} %bitcast_add_fusion), channel_id=1, source_target_pairs={{0,16},{1,17},{2,18},{3,19},{4,20},{5,21},{6,22},{7,23},{8,24},{9,... | collective-permute-start | bytes 4718600 | tf_op jit(solution)/shard_map/ppermute | solution.py:14
  322.3 2.4 collective-permute-start.2
  348.3 210.0 %all-reduce.13.cloned.1.call-start = ((), (), s32[]{:S(2)}) async-start(), calls=%async_computation.3 | async-start | bytes 3145728 | tf_op jit(solution)/shard_map/psum | solution.py:93
  468.4 12.7 %slice-start.9 = ((s8[9437184]{0:T(1024)(128)(4,1)}), s8[4194304]{0:T(1024)(128)(4,1)S(1)}, s32[]{:S(2)}) async-start(s8[9437184]{0:T(1024)(128)(4,1)} %bitcast.96), calls=%async_computation.15 | async-start | bytes 8388608
  468.4 12.7 %slice-start.10 = ((s8[9437184]{0:T(1024)(128)(4,1)}), s8[4194304]{0:T(1024)(128)(4,1)S(1)}, s32[]{:S(2)}) async-start(s8[9437184]{0:T(1024)(128)(4,1)} %bitcast.96), calls=%async_computation.16 | async-start | bytes 8388608
  483.7 3.5 collective-permute-start.3
  487.2 71.1 %copy-start.5 = (f32[256,1536]{1,0:T(8,128)S(1)}, f32[256,1536]{1,0:T(8,128)}, u32[]{:S(2)}) copy-start(f32[256,1536]{1,0:T(8,128)} %copy-done.4) | copy-start | bytes 4718596
  488.8 259.2 %all-reduce.15.cloned.1.call-start = ((), (), s32[]{:S(2)}) async-start(), calls=%async_computation.4 | async-start | bytes 12582912 | tf_op jit(solution)/shard_map/psum | solution.py:74
  558.3 54.5 %slice-start.3 = ((s8[9437184]{0:T(1024)(128)(4,1)}), s8[4194304]{0:T(1024)(128)(4,1)S(1)}, s32[]{:S(2)}) async-start(s8[9437184]{0:T(1024)(128)(4,1)} %bitcast.91), calls=%async_computation.9 | async-start | bytes 8388608
  558.3 54.5 %slice-start.4 = ((s8[9437184]{0:T(1024)(128)(4,1)}), s8[4194304]{0:T(1024)(128)(4,1)S(1)}, s32[]{:S(2)}) async-start(s8[9437184]{0:T(1024)(128)(4,1)} %bitcast.91), calls=%async_computation.10 | async-start | bytes 8388608
  563.8 36.9 %collective-permute-start.4 = (f32[256,1536]{1,0:T(8,128)S(1)}, f32[256,1536]{1,0:T(8,128)S(1)}, u32[]{:S(2)}, u32[]{:S(2)}) collective-permute-start(f32[256,1536]{1,0:T(8,128)S(1)} %get-tuple-element.6), channel_id=1, source_target_pairs={{0,16},{1,17},{2,18},{3,19},{4,20},{5,21},{6,22},{7,23},{8,24},{9,... | collective-permute-start | bytes 4718600 | tf_op jit(solution)/shard_map/ppermute | solution.py:14
  601.9 2.4 collective-permute-start.5
  628.0 210.0 %all-reduce.17.cloned.1.call-start = ((), (), s32[]{:S(2)}) async-start(), calls=%async_computation.5 | async-start | bytes 3145728 | tf_op jit(solution)/shard_map/psum | solution.py:93
  748.1 12.7 %slice-start.12 = ((s8[9437184]{0:T(1024)(128)(4,1)}), s8[4194304]{0:T(1024)(128)(4,1)S(1)}, s32[]{:S(2)}) async-start(s8[9437184]{0:T(1024)(128)(4,1)} %bitcast.98), calls=%async_computation.18 | async-start | bytes 8388608
  748.1 12.7 %slice-start.13 = ((s8[9437184]{0:T(1024)(128)(4,1)}), s8[4194304]{0:T(1024)(128)(4,1)S(1)}, s32[]{:S(2)}) async-start(s8[9437184]{0:T(1024)(128)(4,1)} %bitcast.98), calls=%async_computation.19 | async-start | bytes 8388608
  763.4 3.5 collective-permute-start.6
  766.9 71.1 %copy-start.2 = (f32[2,256,1536]{2,1,0:T(8,128)S(1)}, f32[2,256,1536]{2,1,0:T(8,128)}, u32[]{:S(2)}) copy-start(f32[2,256,1536]{2,1,0:T(8,128)} %param.4) | copy-start | bytes 9437188
  (14 other events, 80.6 us)
Sparse Core Ops, SparseCore 0:
  69.1 120.7 all-reduce.6
  211.8 69.3 all-reduce.8
  348.4 119.8 all-reduce.10
  488.9 69.3 all-reduce.12
  628.1 119.8 all-reduce.14
  768.6 69.3 all-reduce.16
where the time goes:
time: 852 us; the launch traced here: 849 us
  waiting for transfers between devices  593 us (70%)
  other arithmetic  93.2 us (11%)
  local copies, waits for them, and re-layouts  77.4 us (9%)
  matrix products  68.1 us (8%)
  between operations  13.8 us (2%)
    psum x3, waiting for transfers between devices, local(): hidden_grad = lax.psum(partial_hidden, 'wid')  299 us
    psum x3, waiting for transfers between devices, local(): result = own_in + lax.psum(partial_value, 'hid')  208 us
    ppermute x2, waiting for transfers between devices, from_behind(): return lax.ppermute(block, axis, route)  70.8 us
    slice x2, local copies, waits for them, and re-layouts, local(): in_low = jnp.where(is_down, tile_in[:, :half_tile], in_view[:quarter])  27.9 us
    another operation x1, local copies, waits for them, and re-layouts, local(): out_view = tile_out.reshape(half_tile, 2 * quarter)  27.3 us
    select_n x3, other arithmetic, local(): jnp.where(is_down, jnp.concatenate([low_hidden, high_hidden], axis=1), up...  23.4 us
    convert_element_type x3, other arithmetic, local(): hidden = (hidden_grad * gelu_slope(pre_now)).astype(jnp.bfloat16)  21.6 us
    dot_general x3, matrix products, local(): lax.dot_general(second_in, out_high, contract, preferred_element_type=jnp...  21.4 us
  transfers between devices with their start and end apart: 13, of which 13 were waited for; matrix products, arithmetic and copies ran while one was open for 7% of the time, Pallas kernels for 0%

commit v1 on v0

v1 whole, which is shorter than its diff:
```python
import functools

import jax
import jax.numpy as jnp
from jax import lax
from jax.experimental import pallas as pl
from jax.experimental.pallas import tpu as pltpu
from jax.sharding import PartitionSpec as P

CHUNKS = 4
PARTS = 4
LIMIT = 40 * 1024 * 1024
NT = (((1,), (1,)), ((), ()))
LOW = jnp.bfloat16
F32 = jnp.float32


def gelu_slope(pre):
    normal_cdf = 0.5 * (1.0 + jax.scipy.special.erf(pre * 0.7071067811865476))
    density = jnp.exp(-0.5 * pre * pre) * 0.3989422804014327
    return normal_cdf + pre * density


def nt_dot(rows, block):
    return lax.dot_general(rows, block, NT, preferred_element_type=F32)


def params(limit=LIMIT):
    return pltpu.CompilerParams(
        vmem_limit_bytes=limit, dimension_semantics=("arbitrary",)
    )


def first_product(scalars, lhs, lhs_at, tokens, mat, block, place, steps, out_shape, out_block, out_map):
    depth = lhs.shape[1]

    def body(s, lhs_ref, mat_ref, out_ref):
        @pl.when(s[0] == 1)
        def _():
            got = nt_dot(lhs_ref[...].astype(LOW), mat_ref[...])
            out_ref[...] = got.reshape(out_ref.shape).astype(out_ref.dtype)

    return pl.pallas_call(
        body,
        grid_spec=pltpu.PrefetchScalarGridSpec(
            num_scalar_prefetch=1,
            grid=(steps,),
            in_specs=[
                pl.BlockSpec((tokens, depth), lambda i, s: (lhs_at, 0)),
                pl.BlockSpec(block, lambda i, s: place(i * s[0], s)),
            ],
            out_specs=pl.BlockSpec(out_block, lambda i, s: out_map(i * s[0])),
        ),
        out_shape=out_shape,
        compiler_params=params(),
        cost_estimate=pl.CostEstimate(
            flops=2 * tokens * block[0] * block[1] * steps,
            bytes_accessed=2 * block[0] * block[1] * steps,
            transcendentals=0,
        ),
    )(scalars, lhs, mat)


def hidden_product(scalars, lhs, lhs_at, tokens, mat, block, place, steps, base):
    depth = lhs.shape[1]
    width = block[0]

    def body(s, lhs_ref, mat_ref, base_ref, full_ref, low_ref):
        @pl.when(s[0] == 1)
        def _():
            got = nt_dot(lhs_ref[...].astype(LOW), mat_ref[...])
            got = got + base_ref[...].astype(F32)
            full_ref[...] = got
            low_ref[...] = got.astype(LOW)

    spec = pl.BlockSpec((tokens, width), lambda i, s: (0, i * s[0]))
    return pl.pallas_call(
        body,
        grid_spec=pltpu.PrefetchScalarGridSpec(
            num_scalar_prefetch=1,
            grid=(steps,),
            in_specs=[
                pl.BlockSpec((tokens, depth), lambda i, s: (lhs_at, 0)),
                pl.BlockSpec(block, lambda i, s: place(i * s[0], s)),
                spec,
            ],
            out_specs=[spec, spec],
        ),
        out_shape=[
            jax.ShapeDtypeStruct((tokens, width * steps), F32),
            jax.ShapeDtypeStruct((tokens, width * steps), LOW),
        ],
        compiler_params=params(),
        cost_estimate=pl.CostEstimate(
            flops=2 * tokens * block[0] * block[1] * steps,
            bytes_accessed=2 * block[0] * block[1] * steps,
            transcendentals=0,
        ),
    )(scalars, lhs, mat, base)


def back_product(scalars, lhs, mat, block, place, base):
    tokens, depth = lhs.shape
    width = block[0]

    def part_of(i, s):
        return lax.bitwise_xor(s[2], lax.rem(i + 1, PARTS)) * s[0]

    def body(s, lhs_ref, mat_ref, base_ref, one_ref, two_ref, three_ref, own_ref):
        i = pl.program_id(0)

        @pl.when(s[0] == 1)
        def _():
            got = nt_dot(lhs_ref[...], mat_ref[...])
            got = got + base_ref[0].astype(F32)
            for slot, ref in enumerate((one_ref, two_ref, three_ref, own_ref)):

                @pl.when(i == slot)
                def _(ref=ref):
                    ref[...] = got.astype(ref.dtype)

    spec = pl.BlockSpec((tokens, width), lambda i, s: (0, 0))
    return pl.pallas_call(
        body,
        grid_spec=pltpu.PrefetchScalarGridSpec(
            num_scalar_prefetch=1,
            grid=(PARTS,),
            in_specs=[
                pl.BlockSpec((tokens, depth), lambda i, s: (0, 0)),
                pl.BlockSpec(block, lambda i, s: place(part_of(i, s), s)),
                pl.BlockSpec((1, tokens, width), lambda i, s: (part_of(i, s), 0, 0)),
            ],
            out_specs=[spec] * 4,
        ),
        out_shape=[jax.ShapeDtypeStruct((tokens, width), LOW)] * 3
        + [jax.ShapeDtypeStruct((tokens, width), F32)],
        compiler_params=params(),
        cost_estimate=pl.CostEstimate(
            flops=2 * tokens * block[0] * block[1] * PARTS,
            bytes_accessed=2 * block[0] * block[1] * PARTS,
            transcendentals=0,
        ),
    )(scalars, lhs, mat, base)


def split_rows(scalars, mat):
    rows, cols = mat.shape
    step = 256
    half = step // 2

    def body(s, mat_ref, out_ref):
        @pl.when(s[0] == 1)
        def _():
            to = lax.broadcasted_iota(jnp.int32, (step, step), 0)
            source = lax.broadcasted_iota(jnp.int32, (step, step), 1)
            wanted = jnp.where(to < half, 2 * to, 2 * (to - half) + 1)
            pick = jnp.where(source == wanted, 1.0, 0.0).astype(LOW)
            got = jnp.dot(pick, mat_ref[...], preferred_element_type=F32).astype(LOW)
            out_ref[0] = got[:half]
            out_ref[1] = got[half:]

    out = pl.pallas_call(
        body,
        grid_spec=pltpu.PrefetchScalarGridSpec(
            num_scalar_prefetch=1,
            grid=(rows // step,),
            in_specs=[pl.BlockSpec((step, cols), lambda i, s: (i * s[0], 0))],
            out_specs=pl.BlockSpec((2, half, cols), lambda i, s: (0, i * s[0], 0)),
        ),
        out_shape=jax.ShapeDtypeStruct((2, rows // 2, cols), LOW),
        compiler_params=params(),
        cost_estimate=pl.CostEstimate(
            flops=2 * rows * step * cols, bytes_accessed=4 * rows * cols, transcendentals=0
        ),
    )(scalars, mat)
    return out.reshape(rows, cols)


def between_sections(scalars, grad, at, tokens, own, others):
    width = own.shape[1]

    def body(s, grad_ref, own_ref, one_ref, two_ref, three_ref, full_ref, low_ref):
        for slot, ref in enumerate((own_ref, one_ref, two_ref, three_ref)):
            start = pl.multiple_of(lax.bitwise_xor(s[2], slot) * width, 128)
            cols = pl.ds(start, width)
            total = grad_ref[:, cols] + ref[...].astype(F32)
            full_ref[:, cols] = total
            low_ref[:, cols] = total.astype(LOW)

    part = pl.BlockSpec((tokens, width), lambda i, s: (0, 0))
    whole = pl.BlockSpec((tokens, PARTS * width), lambda i, s: (0, 0))
    return pl.pallas_call(
        body,
        grid_spec=pltpu.PrefetchScalarGridSpec(
            num_scalar_prefetch=1,
            grid=(1,),
            in_specs=[pl.BlockSpec((tokens, PARTS * width), lambda i, s: (at, 0))] + [part] * 4,
            out_specs=[whole, whole],
        ),
        out_shape=[
            jax.ShapeDtypeStruct((tokens, PARTS * width), F32),
            jax.ShapeDtypeStruct((tokens, PARTS * width), LOW),
        ],
        compiler_params=params(),
    )(scalars, grad, own, *others)


def finish(scalars, out, between, at, total_tokens, own, others):
    tokens, columns = between.shape
    width = own.shape[1]
    lanes = 128

    def body(s, *refs):
        between_ref, own_ref, one_ref, two_ref, three_ref = refs[:5]
        out_ref, parts_ref = refs[-2:]

        @pl.when(s[0] == 0)
        def _():
            out_ref[...] = between_ref[...]

        @pl.when(s[0] == 1)
        def _():
            for slot, ref in enumerate((own_ref, one_ref, two_ref, three_ref)):
                parts_ref[lax.bitwise_xor(s[2], slot)] = ref[...]
            source = lax.broadcasted_iota(jnp.int32, (2 * lanes, 2 * lanes), 0)
            to = lax.broadcasted_iota(jnp.int32, (2 * lanes, 2 * lanes), 1)
            wanted = jnp.where(source < lanes, 2 * source, 2 * (source - lanes) + 1)
            pick = jnp.where(to == wanted, 1.0, 0.0).astype(LOW)
            for group in range(columns // (2 * lanes)):
                part, inside = divmod(group * lanes, width)
                even = parts_ref[part, :, inside : inside + lanes]
                odd = parts_ref[part + PARTS // 2, :, inside : inside + lanes]
                pair = jnp.concatenate([even, odd], axis=1)
                woven = jnp.dot(pair, pick, preferred_element_type=F32)
                cols = slice(group * 2 * lanes, (group + 1) * 2 * lanes)
                out_ref[:, cols] = between_ref[:, cols] + woven

    part = pl.BlockSpec((tokens, width), lambda i, s: (0, 0))
    earlier = [] if out is None else [out]
    return pl.pallas_call(
        body,
        grid_spec=pltpu.PrefetchScalarGridSpec(
            num_scalar_prefetch=1,
            grid=(1,),
            in_specs=[pl.BlockSpec((tokens, columns), lambda i, s: (0, 0))]
            + [part] * 4
            + [pl.BlockSpec(memory_space=pl.ANY)] * len(earlier),
            out_specs=pl.BlockSpec((tokens, columns), lambda i, s: (at, 0)),
            scratch_shapes=[pltpu.VMEM((PARTS, tokens, width), LOW)],
        ),
        out_shape=jax.ShapeDtypeStruct((total_tokens, columns), F32),
        input_output_aliases={6: 0} if earlier else {},
        compiler_params=params(),
    )(scalars, between, own, *others, *earlier)


def local(grad_out, weight_in, weight_out, pre_act):
    sections = lax.axis_size("section")
    hids = lax.axis_size("hid")
    wids = lax.axis_size("wid")
    section = lax.axis_index("section")
    hid = lax.axis_index("hid")
    wid = lax.axis_index("wid")
    side = wid % 2
    is_up = section == 1

    def scalars(active_section):
        active = (section == active_section).astype(jnp.int32)
        return jnp.stack([active, side, hid % PARTS]).astype(jnp.int32)

    down, up = scalars(0), scalars(1)

    def within(active, distance, axis, block):
        size = lax.axis_size(axis)
        pairs = [(active * size + i, active * size + (i ^ distance)) for i in range(size)]
        return lax.ppermute(block, ("section", axis), pairs)

    def both(distance, axis, block):
        return lax.ppermute(block, axis, [(i, i ^ distance) for i in range(lax.axis_size(axis))])

    mat_in = weight_in[0]
    mat_out = weight_out[0]
    quarter, hid_tile = mat_in.shape
    half = hid_tile // 2
    batches, batch_tokens, _ = grad_out.shape
    total = batches * batch_tokens
    tokens = total // CHUNKS
    grad = grad_out.reshape(total, quarter)
    pre = pre_act[0].reshape(total, hid_tile)
    pre = lax.dynamic_slice_in_dim(pre, side * half, half, 1)

    rows = max(r for r in (512, 384, 256, 128) if half % r == 0)
    per_half = half // rows
    width = quarter // PARTS

    split_out = split_rows(up, mat_out)

    def slope_of(k):
        return lax.optimization_barrier(gelu_slope(pre[k * tokens : (k + 1) * tokens]))

    slopes = [slope_of(k) for k in range(CHUNKS)]

    def reduce_hid(active, parts):
        one, two, three, own = parts
        got = [within(active, d, "hid", part) for d, part in ((1, one), (2, two), (3, three))]
        own = own + got[0].astype(F32) + got[1].astype(F32) + got[2].astype(F32)
        distance = PARTS
        while distance < hids:
            own = own + within(active, distance, "hid", own)
            distance *= 2
        return own.astype(LOW)

    def backward(k, active, flags, hidden_grad, low_grad):
        other = within(active, 2, "wid", low_grad)
        return ((hidden_grad + other.astype(F32)) * slopes[k]).astype(LOW)

    k1 = dict(tokens=tokens, block=(rows, quarter), steps=per_half)

    def down_chunk(k):
        sent = first_product(
            down, grad, k, mat=mat_out, place=lambda i, s: ((1 - s[1]) * s[0] * per_half + i, 0),
            out_shape=jax.ShapeDtypeStruct((tokens, half), LOW),
            out_block=(tokens, rows), out_map=lambda i: (0, i), **k1,
        )
        got = within(0, 1, "wid", sent)
        full, low = hidden_product(
            down, grad, k, mat=mat_out, place=lambda i, s: (s[1] * s[0] * per_half + i, 0),
            base=got, **k1,
        )
        hidden = backward(k, 0, down, full, low)
        swapped = within(0, 1, "wid", hidden)
        partial = first_product(
            down, hidden, 0, tokens=tokens, mat=mat_in, block=(width, half),
            place=lambda i, s: (i, s[1] * s[0]), steps=PARTS,
            out_shape=jax.ShapeDtypeStruct((PARTS, tokens, width), F32),
            out_block=(1, tokens, width), out_map=lambda i: (i, 0, 0),
        )
        parts = back_product(
            down, swapped, mat_in, (width, half),
            lambda part, s: (part, (1 - s[1]) * s[0]), partial,
        )
        term = reduce_hid(0, parts)
        crossed = lax.ppermute(term, "section", [(0, 1)])
        term = jnp.where(is_up, crossed, term)
        others = [both(d, "hid", term) for d in (1, 2, 3)]
        return between_sections(up, grad, k, tokens, term, others)

    def up_chunk(k, out, between, low):
        low_other = within(1, 1, "wid", low)
        partial = first_product(
            up, low, 0, mat=split_out, place=lambda i, s: (s[1] * s[0] * per_half + i, 0),
            out_shape=jax.ShapeDtypeStruct((tokens, half), F32),
            out_block=(tokens, rows), out_map=lambda i: (0, i), **k1,
        )
        full, low_grad = hidden_product(
            up, low_other, 0, mat=split_out,
            place=lambda i, s: ((1 - s[1]) * s[0] * per_half + i, 0), base=partial, **k1,
        )
        hidden = backward(k, 1, up, full, low_grad)

        def place(core, part):
            return core * (PARTS // 2) + part % (PARTS // 2), part // (PARTS // 2)

        sent = first_product(
            up, hidden, 0, tokens=tokens, mat=mat_in, block=(width, half),
            place=lambda i, s: place((1 - s[1]) * s[0], i), steps=PARTS,
            out_shape=jax.ShapeDtypeStruct((PARTS, tokens, width), LOW),
            out_block=(1, tokens, width), out_map=lambda i: (i, 0, 0),
        )
        got = within(1, 1, "wid", sent)
        parts = back_product(
            up, hidden, mat_in, (width, half),
            lambda part, s: place(s[1] * s[0], part), got,
        )
        term = reduce_hid(1, parts)
        others = [within(1, d, "hid", term) for d in (1, 2, 3)]
        return finish(up, out, between, k, total, term, others)

    firsts = [down_chunk(k) for k in range(CHUNKS)]
    out = None
    for k in range(CHUNKS):
        out = up_chunk(k, out, *firsts[k])
    return out.reshape(1, batches, batch_tokens, quarter)


def solution(mesh):
    return jax.shard_map(
        local,
        mesh=mesh,
        in_specs=(
            P(None, None, "wid"),
            P("section", "wid", "hid"),
            P("section", "hid", "wid"),
            P("section", None, None, "hid"),
        ),
        out_specs=P("section", None, None, "wid"),
        check_vma=False,
    )
```

time: 852 us -> 511 us (0.60)
  waiting for transfers between devices: 593 us -> 143 us
  Pallas kernels: 0 us -> 188 us
  starting transfers between devices: 3.46 us -> 162 us
  other arithmetic: 93.2 us -> 9.81 us
  local copies, waits for them, and re-layouts: 77.4 us -> 2.77 us
  matrix products: 68.1 us -> 0 us
  between operations: 13.8 us -> 1.29 us
    psum x6 -> x0, waiting for transfers between devices: 508 us -> none  [the longest x3 299 us: local(): hidden_grad = lax.psum(partial_hidden, 'wid')]
    pallas_call x0 -> x41, Pallas kernels: none -> 188 us  [the longest x16 76.8 us: first_product(): pl.pallas_call(body, grid_spec=pltpu.PrefetchScalarGridSpec(num_scalar_pr...]
    ppermute x7 -> x76, starting transfers between devices: 3.25 us -> 162 us  [the longest x60 129 us: within(): return lax.ppermute(block, ('section', axis), pairs)]
    dot_general x12 -> x0, matrix products: 68.1 us -> none  [the longest x3 21.4 us: local(): lax.dot_general(second_in, out_high, contract, preferred_element_type=jnp...]
    ppermute x7 -> x76, waiting for transfers between devices: 85.8 us -> 143 us  [the longest x4 134 us: down_chunk(): crossed = lax.ppermute(term, 'section', [(0, 1)])]
    select_n x5 -> x4, other arithmetic: 56 us -> 0.07 us  [down_chunk(): term = jnp.where(is_up, crossed, term)]
    slice x3 -> x0, local copies, waits for them, and re-layouts: 41.6 us -> none  [the longest x2 27.9 us: local(): in_low = jnp.where(is_down, tile_in[:, :half_tile], in_view[:quarter])]
    another operation x1 -> x0, local copies, waits for them, and re-layouts: 27.3 us -> none  [local(): out_view = tile_out.reshape(half_tile, 2 * quarter)]
  transfers between devices with their start and end apart: 13 -> 76, of which waited for: 13 -> 5; matrix products, arithmetic and copies ran while one was open for 7% -> 2% of each run, Pallas kernels for 0% -> 36%
where the time goes in v1:
time: 511 us; the launch traced here: 508 us
  Pallas kernels  188 us (37%)
  starting transfers between devices  162 us (32%)
  waiting for transfers between devices  143 us (28%)
  other arithmetic  9.81 us (2%)
    ppermute x4, waiting for transfers between devices, down_chunk(): crossed = lax.ppermute(term, 'section', [(0, 1)])  134 us
    ppermute x60, starting transfers between devices, within(): return lax.ppermute(block, ('section', axis), pairs)  129 us
    pallas_call x16, Pallas kernels, first_product(): pl.pallas_call(body, grid_spec=pltpu.PrefetchScalarGridSpec(num_scalar_pr...  76.8 us
    pallas_call x8, Pallas kernels, hidden_product(): pl.pallas_call(body, grid_spec=pltpu.PrefetchScalarGridSpec(num_scalar_pr...  39.7 us
    pallas_call x8, Pallas kernels, back_product(): pl.pallas_call(body, grid_spec=pltpu.PrefetchScalarGridSpec(num_scalar_pr...  35.8 us
    ppermute x12, starting transfers between devices, both(): lax.ppermute(block, axis, [(i, i ^ distance) for i in range(lax.axis_size...  28.6 us
    pallas_call x1, Pallas kernels, split_rows(): pl.pallas_call(body, grid_spec=pltpu.PrefetchScalarGridSpec(num_scalar_pr...  26.3 us
  transfers between devices with their start and end apart: 76, of which 5 were waited for; matrix products, arithmetic and copies ran while one was open for 2% of the time, Pallas kernels for 36%

profile of v1, /device:TPU:2, one launch (start us, length us, event | category | flops | bytes accessed | tf_op | source)
XLA Modules:
  0.0 507.7 jit_solution(13055842941265075815)
XLA Ops:
  18.7 7.2 %fusion.15 = (f32[128,3072]{1,0:T(8,128)}, f32[128,3072]{1,0:T(8,128)}, f32[128,3072]{1,0:T(8,128)}, f32[128,3072]{1,0:T(8,128)}) fusion(f32[512,6144]{1,0:T(8,128)} %bitcast.55, s32[]{:T(128)S(6)} %select_n.39, s32[]{:T(128)S(6)} %add.180, s32[]{:T(128)S(6)} %add.179, s32[]{:T(128)S(6)} %add.178), kind=kLoop, calls=%fused_computation.19 | loop fusion | flops 12582912 | bytes 12582928 | tf_op jit(solution)/shard_map/add | solution.py:21
  28.7 26.3 %shard_map.51 = bf16[2,3072,1536]{2,1,0:T(8,128)(2,1)} custom-call(s32[3]{0:T(128)S(1)} %add_add_fusion.s, bf16[6144,1536]{1,0:T(8,128)(2,1)} %bitcast.43), custom_call_target="tpu_custom_call" | custom-call | flops 4831838208 | bytes 37748736 | tf_op jit(solution)/shard_map/pallas_call | solution.py:162
  97.6 134.4 %collective-permute-done.6 = bf16[128,384]{1,0:T(8,128)(2,1)S(1)} collective-permute-done((bf16[128,384]{1,0:T(8,128)(2,1)S(1)}, bf16[128,384]{1,0:T(8,128)(2,1)S(1)}, u32[]{:S(2)}, u32[]{:S(2)}) %collective-permute-start.6) | collective-permute-done | bytes 98336 | tf_op jit(solution)/shard_map/ppermute | solution.py:343
  251.2 7.7 %shard_map.52.base_ref = f32[128,3072]{1,0:T(8,128)S(1)} custom-call(s32[3]{0:T(128)S(1)} %add_add_fusion.s, bf16[128,1536]{1,0:T(8,128)(2,1)S(1)} %get-tuple-element.68.lhs_ref, bf16[6144,1536]{1,0:T(8,128)(2,1)} %bitcast.47), custom_call_target="tpu_custom_call" | custom-call | flops 1207959552 | bytes 9437184 | tf_op jit(solution)/shard_map/pallas_call | solution.py:43
  262.6 7.9 %shard_map.53 = (f32[128,3072]{1,0:T(8,128)S(1)}, bf16[128,3072]{1,0:T(8,128)(2,1)S(1)}) custom-call(s32[3]{0:T(128)S(1)} %add_add_fusion.s, bf16[128,1536]{1,0:T(8,128)(2,1)S(1)} %collective-permute-done.10.lhs_ref, bf16[6144,1536]{1,0:T(8,128)(2,1)} %bitcast.48, f32[128,3072]{1,0:T(8,128)S(1)} %shard_map.52.base_ref), custom_call_target="tpu_custom_call" | custom-call | flops 1207959552 | bytes 9437184 | tf_op jit(solution)/shard_map/pallas_call | solution.py:77
  270.5 5.8 %collective-permute-start.46 = (bf16[128,384]{1,0:T(8,128)(2,1)S(1)}, bf16[128,384]{1,0:T(8,128)(2,1)S(1)}, u32[]{:S(2)}, u32[]{:S(2)}) collective-permute-start(bf16[128,384]{1,0:T(8,128)(2,1)S(1)} %broadcast_select_fusion.1.own_ref), channel_id=1, source_target_pairs={{0,8},{4,12},{8,0},{12,4},{1,9},{5,13},{9,1},{13,5},{2,10},{6,14},... | collective-permute-start | bytes 294920 | tf_op jit(solution)/shard_map/ppermute | solution.py:279
  276.3 5.7 %collective-permute-start.47 = (bf16[128,384]{1,0:T(8,128)(2,1)S(1)}, bf16[128,384]{1,0:T(8,128)(2,1)S(1)}, u32[]{:S(2)}, u32[]{:S(2)}) collective-permute-start(bf16[128,384]{1,0:T(8,128)(2,1)S(1)} %broadcast_select_fusion.1.own_ref), channel_id=1, source_target_pairs={{0,12},{4,8},{8,4},{12,0},{1,13},{5,9},{9,5},{13,1},{2,14},{6,10},... | collective-permute-start | bytes 294920 | tf_op jit(solution)/shard_map/ppermute | solution.py:279
  295.1 7.7 %shard_map.61.base_ref = f32[128,3072]{1,0:T(8,128)S(1)} custom-call(s32[3]{0:T(128)S(1)} %add_add_fusion.s, bf16[128,1536]{1,0:T(8,128)(2,1)S(1)} %get-tuple-element.82.lhs_ref, bf16[6144,1536]{1,0:T(8,128)(2,1)} %bitcast.49), custom_call_target="tpu_custom_call" | custom-call | flops 1207959552 | bytes 9437184 | tf_op jit(solution)/shard_map/pallas_call | solution.py:43
  306.0 7.7 %shard_map.70.base_ref = f32[128,3072]{1,0:T(8,128)S(1)} custom-call(s32[3]{0:T(128)S(1)} %add_add_fusion.s, bf16[128,1536]{1,0:T(8,128)(2,1)S(1)} %get-tuple-element.96.lhs_ref, bf16[6144,1536]{1,0:T(8,128)(2,1)} %bitcast.50), custom_call_target="tpu_custom_call" | custom-call | flops 1207959552 | bytes 9437184 | tf_op jit(solution)/shard_map/pallas_call | solution.py:43
  313.7 7.7 %shard_map.79.base_ref = f32[128,3072]{1,0:T(8,128)S(1)} custom-call(s32[3]{0:T(128)S(1)} %add_add_fusion.s, bf16[128,1536]{1,0:T(8,128)(2,1)S(1)} %get-tuple-element.110.lhs_ref, bf16[6144,1536]{1,0:T(8,128)(2,1)} %bitcast.51), custom_call_target="tpu_custom_call" | custom-call | flops 1207959552 | bytes 9437184 | tf_op jit(solution)/shard_map/pallas_call | solution.py:43
  321.4 7.9 %shard_map.62 = (f32[128,3072]{1,0:T(8,128)S(1)}, bf16[128,3072]{1,0:T(8,128)(2,1)S(1)}) custom-call(s32[3]{0:T(128)S(1)} %add_add_fusion.s, bf16[128,1536]{1,0:T(8,128)(2,1)S(1)} %collective-permute-done.29.lhs_ref, bf16[6144,1536]{1,0:T(8,128)(2,1)} %bitcast.52, f32[128,3072]{1,0:T(8,128)S(1)} %shard_map.61.base_ref), custom_call_target="tpu_custom_call" | custom-call | flops 1207959552 | bytes 9437184 | tf_op jit(solution)/shard_map/pallas_call | solution.py:77
  331.8 7.9 %shard_map.71 = (f32[128,3072]{1,0:T(8,128)S(1)}, bf16[128,3072]{1,0:T(8,128)(2,1)S(1)}) custom-call(s32[3]{0:T(128)S(1)} %add_add_fusion.s, bf16[128,1536]{1,0:T(8,128)(2,1)S(1)} %collective-permute-done.48.lhs_ref, bf16[6144,1536]{1,0:T(8,128)(2,1)} %bitcast.53, f32[128,3072]{1,0:T(8,128)S(1)} %shard_map.70.base_ref), custom_call_target="tpu_custom_call" | custom-call | flops 1207959552 | bytes 9437184 | tf_op jit(solution)/shard_map/pallas_call | solution.py:77
  343.2 7.9 %shard_map.80 = (f32[128,3072]{1,0:T(8,128)S(1)}, bf16[128,3072]{1,0:T(8,128)(2,1)S(1)}) custom-call(s32[3]{0:T(128)S(1)} %add_add_fusion.s, bf16[128,1536]{1,0:T(8,128)(2,1)S(1)} %collective-permute-done.67.lhs_ref, bf16[6144,1536]{1,0:T(8,128)(2,1)} %bitcast.54, f32[128,3072]{1,0:T(8,128)S(1)} %shard_map.79.base_ref), custom_call_target="tpu_custom_call" | custom-call | flops 1207959552 | bytes 9437184 | tf_op jit(solution)/shard_map/pallas_call | solution.py:77
  353.9 6.6 %shard_map.54 = bf16[4,128,384]{2,1,0:T(8,128)(2,1)S(1)} custom-call(s32[3]{0:T(128)S(1)} %add_add_fusion.s, bf16[128,3072]{1,0:T(8,128)(2,1)S(1)} %multiply_convert_fusion.6.lhs_ref, bf16[1536,6144]{1,0:T(8,128)(2,1)} %bitcast.30), custom_call_target="tpu_custom_call" | custom-call | flops 1207959552 | bytes 9437184 | tf_op jit(solution)/shard_map/pallas_call | solution.py:43
  362.8 6.6 %shard_map.63 = bf16[4,128,384]{2,1,0:T(8,128)(2,1)S(1)} custom-call(s32[3]{0:T(128)S(1)} %add_add_fusion.s, bf16[128,3072]{1,0:T(8,128)(2,1)S(1)} %multiply_convert_fusion.4.lhs_ref, bf16[1536,6144]{1,0:T(8,128)(2,1)} %bitcast.31), custom_call_target="tpu_custom_call" | custom-call | flops 1207959552 | bytes 9437184 | tf_op jit(solution)/shard_map/pallas_call | solution.py:43
  372.1 6.6 %shard_map.72 = bf16[4,128,384]{2,1,0:T(8,128)(2,1)S(1)} custom-call(s32[3]{0:T(128)S(1)} %add_add_fusion.s, bf16[128,3072]{1,0:T(8,128)(2,1)S(1)} %multiply_convert_fusion.2.lhs_ref, bf16[1536,6144]{1,0:T(8,128)(2,1)} %bitcast.32), custom_call_target="tpu_custom_call" | custom-call | flops 1207959552 | bytes 9437184 | tf_op jit(solution)/shard_map/pallas_call | solution.py:43
  384.6 6.6 %shard_map.81 = bf16[4,128,384]{2,1,0:T(8,128)(2,1)S(1)} custom-call(s32[3]{0:T(128)S(1)} %add_add_fusion.s, bf16[128,3072]{1,0:T(8,128)(2,1)S(1)} %multiply_convert_fusion.lhs_ref, bf16[1536,6144]{1,0:T(8,128)(2,1)} %bitcast.33), custom_call_target="tpu_custom_call" | custom-call | flops 1207959552 | bytes 9437184 | tf_op jit(solution)/shard_map/pallas_call | solution.py:43
  393.2 6.7 %shard_map.55 = (bf16[128,384]{1,0:T(8,128)(2,1)S(1)}, bf16[128,384]{1,0:T(8,128)(2,1)S(1)}, bf16[128,384]{1,0:T(8,128)(2,1)S(1)}, f32[128,384]{1,0:T(8,128)S(1)}) custom-call(s32[3]{0:T(128)S(1)} %add_add_fusion.s, bf16[128,3072]{1,0:T(8,128)(2,1)S(1)} %multiply_convert_fusion.6.lhs_ref, bf16[1536,6144]{1,0:T(8,128)(2,1)} %bitcast.34, ...), custom_call_target="tpu_custom_call" | custom-call | flops 1207959552 | bytes 9437184 | tf_op jit(solution)/shard_map/pallas_call | solution.py:123
  399.9 5.3 %collective-permute-start.15 = (bf16[128,384]{1,0:T(8,128)(2,1)S(1)}, bf16[128,384]{1,0:T(8,128)(2,1)S(1)}, u32[]{:S(2)}, u32[]{:S(2)}) collective-permute-start(bf16[128,384]{1,0:T(8,128)(2,1)S(1)} %get-tuple-element.74), channel_id=1, source_target_pairs={{16,28},{20,24},{24,20},{28,16},{17,29},{21,25},{25,21},{29,17},{1... | collective-permute-start | bytes 294920 | tf_op jit(solution)/shard_map/ppermute | solution.py:276
  407.2 6.7 %shard_map.64 = (bf16[128,384]{1,0:T(8,128)(2,1)S(1)}, bf16[128,384]{1,0:T(8,128)(2,1)S(1)}, bf16[128,384]{1,0:T(8,128)(2,1)S(1)}, f32[128,384]{1,0:T(8,128)S(1)}) custom-call(s32[3]{0:T(128)S(1)} %add_add_fusion.s, bf16[128,3072]{1,0:T(8,128)(2,1)S(1)} %multiply_convert_fusion.4.lhs_ref, bf16[1536,6144]{1,0:T(8,128)(2,1)} %bitcast.35, ...), custom_call_target="tpu_custom_call" | custom-call | flops 1207959552 | bytes 9437184 | tf_op jit(solution)/shard_map/pallas_call | solution.py:123
  420.7 6.7 %shard_map.73 = (bf16[128,384]{1,0:T(8,128)(2,1)S(1)}, bf16[128,384]{1,0:T(8,128)(2,1)S(1)}, bf16[128,384]{1,0:T(8,128)(2,1)S(1)}, f32[128,384]{1,0:T(8,128)S(1)}) custom-call(s32[3]{0:T(128)S(1)} %add_add_fusion.s, bf16[128,3072]{1,0:T(8,128)(2,1)S(1)} %multiply_convert_fusion.2.lhs_ref, bf16[1536,6144]{1,0:T(8,128)(2,1)} %bitcast.36, ...), custom_call_target="tpu_custom_call" | custom-call | flops 1207959552 | bytes 9437184 | tf_op jit(solution)/shard_map/pallas_call | solution.py:123
  431.0 6.7 %shard_map.82 = (bf16[128,384]{1,0:T(8,128)(2,1)S(1)}, bf16[128,384]{1,0:T(8,128)(2,1)S(1)}, bf16[128,384]{1,0:T(8,128)(2,1)S(1)}, f32[128,384]{1,0:T(8,128)S(1)}) custom-call(s32[3]{0:T(128)S(1)} %add_add_fusion.s, bf16[128,3072]{1,0:T(8,128)(2,1)S(1)} %multiply_convert_fusion.lhs_ref, bf16[1536,6144]{1,0:T(8,128)(2,1)} %bitcast.37, ...), custom_call_target="tpu_custom_call" | custom-call | flops 1207959552 | bytes 9437184 | tf_op jit(solution)/shard_map/pallas_call | solution.py:123
  443.6 4.3 collective-permute-start.51
  476.7 4.3 collective-permute-start.74
  (208 shorter events, 197.3 us)
Async XLA Ops:
  8.8 46.3 %collective-permute-start.19 = (bf16[128,3072]{1,0:T(8,128)(2,1)}, bf16[128,3072]{1,0:T(8,128)(2,1)}, u32[]{:S(2)}, u32[]{:S(2)}) collective-permute-start(bf16[128,3072]{1,0:T(8,128)(2,1)} %shard_map.56), channel_id=1, source_target_pairs={{0,1},{1,0},{2,3},{3,2},{4,5},{5,4},{6,7},{7,6},{8,9},{9,8},{10,11... | collective-permute-start | bytes 2359304 | tf_op jit(solution)/shard_map/ppermute | solution.py:276
  12.9 44.9 %collective-permute-start.38 = (bf16[128,3072]{1,0:T(8,128)(2,1)}, bf16[128,3072]{1,0:T(8,128)(2,1)}, u32[]{:S(2)}, u32[]{:S(2)}) collective-permute-start(bf16[128,3072]{1,0:T(8,128)(2,1)} %shard_map.65), channel_id=1, source_target_pairs={{0,1},{1,0},{2,3},{3,2},{4,5},{5,4},{6,7},{7,6},{8,9},{9,8},{10,11... | collective-permute-start | bytes 2359304 | tf_op jit(solution)/shard_map/ppermute | solution.py:276
  17.1 43.6 %collective-permute-start.57 = (bf16[128,3072]{1,0:T(8,128)(2,1)}, bf16[128,3072]{1,0:T(8,128)(2,1)}, u32[]{:S(2)}, u32[]{:S(2)}) collective-permute-start(bf16[128,3072]{1,0:T(8,128)(2,1)} %shard_map.74), channel_id=1, source_target_pairs={{0,1},{1,0},{2,3},{3,2},{4,5},{5,4},{6,7},{7,6},{8,9},{9,8},{10,11... | collective-permute-start | bytes 2359304 | tf_op jit(solution)/shard_map/ppermute | solution.py:276
  28.0 35.5 %collective-permute-start.1 = (bf16[128,3072]{1,0:T(8,128)(2,1)S(1)}, bf16[128,3072]{1,0:T(8,128)(2,1)S(1)}, u32[]{:S(2)}, u32[]{:S(2)}) collective-permute-start(bf16[128,3072]{1,0:T(8,128)(2,1)S(1)} %get-tuple-element.62), channel_id=1, source_target_pairs={{0,2},{1,3},{2,0},{3,1},{4,6},{5,7},{6,4},{7,5},{8,10},{9,11},{10,... | collective-permute-start | bytes 2359304 | tf_op jit(solution)/shard_map/ppermute | solution.py:276
  92.8 140.5 %collective-permute-start.62 = (bf16[128,384]{1,0:T(8,128)(2,1)S(1)}, bf16[128,384]{1,0:T(8,128)(2,1)S(1)}, u32[]{:S(2)}, u32[]{:S(2)}) collective-permute-start(bf16[128,384]{1,0:T(8,128)(2,1)S(1)} %get-tuple-element.108), channel_id=1, source_target_pairs={{0,12},{4,8},{8,4},{12,0},{1,13},{5,9},{9,5},{13,1},{2,14},{6,10},... | collective-permute-start | bytes 294920 | tf_op jit(solution)/shard_map/ppermute | solution.py:276
  93.5 141.3 %collective-permute-start.61 = (bf16[128,384]{1,0:T(8,128)(2,1)S(1)}, bf16[128,384]{1,0:T(8,128)(2,1)S(1)}, u32[]{:S(2)}, u32[]{:S(2)}) collective-permute-start(bf16[128,384]{1,0:T(8,128)(2,1)S(1)} %get-tuple-element.107), channel_id=1, source_target_pairs={{0,8},{4,12},{8,0},{12,4},{1,9},{5,13},{9,1},{13,5},{2,10},{6,14},... | collective-permute-start | bytes 294920 | tf_op jit(solution)/shard_map/ppermute | solution.py:276
  94.2 143.5 %collective-permute-start.60 = (bf16[128,384]{1,0:T(8,128)(2,1)S(1)}, bf16[128,384]{1,0:T(8,128)(2,1)S(1)}, u32[]{:S(2)}, u32[]{:S(2)}) collective-permute-start(bf16[128,384]{1,0:T(8,128)(2,1)S(1)} %get-tuple-element.106), channel_id=1, source_target_pairs={{0,4},{4,0},{8,12},{12,8},{1,5},{5,1},{9,13},{13,9},{2,6},{6,2},{1... | collective-permute-start | bytes 294920 | tf_op jit(solution)/shard_map/ppermute | solution.py:276
  94.9 137.0 %collective-permute-start.6 = (bf16[128,384]{1,0:T(8,128)(2,1)S(1)}, bf16[128,384]{1,0:T(8,128)(2,1)S(1)}, u32[]{:S(2)}, u32[]{:S(2)}) collective-permute-start(bf16[128,384]{1,0:T(8,128)(2,1)S(1)} %add_convert_fusion.7), channel_id=1, source_target_pairs={{0,16},{1,17},{2,18},{3,19},{4,20},{5,21},{6,22},{7,23},{8,24},{9,... | collective-permute-start | bytes 294920 | tf_op jit(solution)/shard_map/ppermute | solution.py:343
  96.2 150.5 %collective-permute-start.25 = (bf16[128,384]{1,0:T(8,128)(2,1)S(1)}, bf16[128,384]{1,0:T(8,128)(2,1)S(1)}, u32[]{:S(2)}, u32[]{:S(2)}) collective-permute-start(bf16[128,384]{1,0:T(8,128)(2,1)S(1)} %add_convert_fusion.5), channel_id=1, source_target_pairs={{0,16},{1,17},{2,18},{3,19},{4,20},{5,21},{6,22},{7,23},{8,24},{9,... | collective-permute-start | bytes 294920 | tf_op jit(solution)/shard_map/ppermute | solution.py:343
  246.8 35.2 %collective-permute-start.27 = (bf16[128,384]{1,0:T(8,128)(2,1)S(1)}, bf16[128,384]{1,0:T(8,128)(2,1)S(1)}, u32[]{:S(2)}, u32[]{:S(2)}) collective-permute-start(bf16[128,384]{1,0:T(8,128)(2,1)S(1)} %broadcast_select_fusion.2.own_ref), channel_id=1, source_target_pairs={{0,8},{4,12},{8,0},{12,4},{1,9},{5,13},{9,1},{13,5},{2,10},{6,14},... | collective-permute-start | bytes 294920 | tf_op jit(solution)/shard_map/ppermute | solution.py:279
  248.5 36.9 %collective-permute-start.28 = (bf16[128,384]{1,0:T(8,128)(2,1)S(1)}, bf16[128,384]{1,0:T(8,128)(2,1)S(1)}, u32[]{:S(2)}, u32[]{:S(2)}) collective-permute-start(bf16[128,384]{1,0:T(8,128)(2,1)S(1)} %broadcast_select_fusion.2.own_ref), channel_id=1, source_target_pairs={{0,12},{4,8},{8,4},{12,0},{1,13},{5,9},{9,5},{13,1},{2,14},{6,10},... | collective-permute-start | bytes 294920 | tf_op jit(solution)/shard_map/ppermute | solution.py:279
  282.0 71.6 %collective-permute-start.11 = (bf16[128,3072]{1,0:T(8,128)(2,1)S(1)}, bf16[128,3072]{1,0:T(8,128)(2,1)S(1)}, u32[]{:S(2)}, u32[]{:S(2)}) collective-permute-start(bf16[128,3072]{1,0:T(8,128)(2,1)S(1)} %get-tuple-element.70), channel_id=1, source_target_pairs={{16,18},{17,19},{18,16},{19,17},{20,22},{21,23},{22,20},{23,21},{2... | collective-permute-start | bytes 2359304 | tf_op jit(solution)/shard_map/ppermute | solution.py:276
  287.6 33.8 %collective-permute-start.29 = (bf16[128,1536]{1,0:T(8,128)(2,1)S(1)}, bf16[128,1536]{1,0:T(8,128)(2,1)S(1)}, u32[]{:S(2)}, u32[]{:S(2)}) collective-permute-start(bf16[128,1536]{1,0:T(8,128)(2,1)S(1)} %get-tuple-element.82.lhs_ref), channel_id=1, source_target_pairs={{16,17},{17,16},{18,19},{19,18},{20,21},{21,20},{22,23},{23,22},{2... | collective-permute-start | bytes 1179656 | tf_op jit(solution)/shard_map/ppermute | solution.py:276
  293.2 38.6 %collective-permute-start.48 = (bf16[128,1536]{1,0:T(8,128)(2,1)S(1)}, bf16[128,1536]{1,0:T(8,128)(2,1)S(1)}, u32[]{:S(2)}, u32[]{:S(2)}) collective-permute-start(bf16[128,1536]{1,0:T(8,128)(2,1)S(1)} %get-tuple-element.96.lhs_ref), channel_id=1, source_target_pairs={{16,17},{17,16},{18,19},{19,18},{20,21},{21,20},{22,23},{23,22},{2... | collective-permute-start | bytes 1179656 | tf_op jit(solution)/shard_map/ppermute | solution.py:276
  303.5 39.7 %collective-permute-start.67 = (bf16[128,1536]{1,0:T(8,128)(2,1)S(1)}, bf16[128,1536]{1,0:T(8,128)(2,1)S(1)}, u32[]{:S(2)}, u32[]{:S(2)}) collective-permute-start(bf16[128,1536]{1,0:T(8,128)(2,1)S(1)} %get-tuple-element.110.lhs_ref), channel_id=1, source_target_pairs={{16,17},{17,16},{18,19},{19,18},{20,21},{21,20},{22,23},{23,22},{2... | collective-permute-start | bytes 1179656 | tf_op jit(solution)/shard_map/ppermute | solution.py:276
  329.3 33.2 %collective-permute-start.30 = (bf16[128,3072]{1,0:T(8,128)(2,1)S(1)}, bf16[128,3072]{1,0:T(8,128)(2,1)S(1)}, u32[]{:S(2)}, u32[]{:S(2)}) collective-permute-start(bf16[128,3072]{1,0:T(8,128)(2,1)S(1)} %get-tuple-element.84), channel_id=1, source_target_pairs={{16,18},{17,19},{18,16},{19,17},{20,22},{21,23},{22,20},{23,21},{2... | collective-permute-start | bytes 2359304 | tf_op jit(solution)/shard_map/ppermute | solution.py:276
  339.7 32.1 %collective-permute-start.49 = (bf16[128,3072]{1,0:T(8,128)(2,1)S(1)}, bf16[128,3072]{1,0:T(8,128)(2,1)S(1)}, u32[]{:S(2)}, u32[]{:S(2)}) collective-permute-start(bf16[128,3072]{1,0:T(8,128)(2,1)S(1)} %get-tuple-element.98), channel_id=1, source_target_pairs={{16,18},{17,19},{18,16},{19,17},{20,22},{21,23},{22,20},{23,21},{2... | collective-permute-start | bytes 2359304 | tf_op jit(solution)/shard_map/ppermute | solution.py:276
  351.2 33.2 %collective-permute-start.68 = (bf16[128,3072]{1,0:T(8,128)(2,1)S(1)}, bf16[128,3072]{1,0:T(8,128)(2,1)S(1)}, u32[]{:S(2)}, u32[]{:S(2)}) collective-permute-start(bf16[128,3072]{1,0:T(8,128)(2,1)S(1)} %get-tuple-element.112), channel_id=1, source_target_pairs={{16,18},{17,19},{18,16},{19,17},{20,22},{21,23},{22,20},{23,21},{2... | collective-permute-start | bytes 2359304 | tf_op jit(solution)/shard_map/ppermute | solution.py:276
  360.6 32.7 %collective-permute-start.12 = (bf16[4,128,384]{2,1,0:T(8,128)(2,1)S(1)}, bf16[4,128,384]{2,1,0:T(8,128)(2,1)S(1)}, u32[]{:S(2)}, u32[]{:S(2)}) collective-permute-start(bf16[4,128,384]{2,1,0:T(8,128)(2,1)S(1)} %shard_map.54), channel_id=1, source_target_pairs={{16,17},{17,16},{18,19},{19,18},{20,21},{21,20},{22,23},{23,22},{2... | collective-permute-start | bytes 1179656 | tf_op jit(solution)/shard_map/ppermute | solution.py:276
  369.4 37.8 %collective-permute-start.31 = (bf16[4,128,384]{2,1,0:T(8,128)(2,1)S(1)}, bf16[4,128,384]{2,1,0:T(8,128)(2,1)S(1)}, u32[]{:S(2)}, u32[]{:S(2)}) collective-permute-start(bf16[4,128,384]{2,1,0:T(8,128)(2,1)S(1)} %shard_map.63), channel_id=1, source_target_pairs={{16,17},{17,16},{18,19},{19,18},{20,21},{21,20},{22,23},{23,22},{2... | collective-permute-start | bytes 1179656 | tf_op jit(solution)/shard_map/ppermute | solution.py:276
  378.7 38.1 %collective-permute-start.50 = (bf16[4,128,384]{2,1,0:T(8,128)(2,1)S(1)}, bf16[4,128,384]{2,1,0:T(8,128)(2,1)S(1)}, u32[]{:S(2)}, u32[]{:S(2)}) collective-permute-start(bf16[4,128,384]{2,1,0:T(8,128)(2,1)S(1)} %shard_map.72), channel_id=1, source_target_pairs={{16,17},{17,16},{18,19},{19,18},{20,21},{21,20},{22,23},{23,22},{2... | collective-permute-start | bytes 1179656 | tf_op jit(solution)/shard_map/ppermute | solution.py:276
  391.3 36.1 %collective-permute-start.69 = (bf16[4,128,384]{2,1,0:T(8,128)(2,1)S(1)}, bf16[4,128,384]{2,1,0:T(8,128)(2,1)S(1)}, u32[]{:S(2)}, u32[]{:S(2)}) collective-permute-start(bf16[4,128,384]{2,1,0:T(8,128)(2,1)S(1)} %shard_map.81), channel_id=1, source_target_pairs={{16,17},{17,16},{18,19},{19,18},{20,21},{21,20},{22,23},{23,22},{2... | collective-permute-start | bytes 1179656 | tf_op jit(solution)/shard_map/ppermute | solution.py:276
  399.9 67.0 %collective-permute-start.15 = (bf16[128,384]{1,0:T(8,128)(2,1)S(1)}, bf16[128,384]{1,0:T(8,128)(2,1)S(1)}, u32[]{:S(2)}, u32[]{:S(2)}) collective-permute-start(bf16[128,384]{1,0:T(8,128)(2,1)S(1)} %get-tuple-element.74), channel_id=1, source_target_pairs={{16,28},{20,24},{24,20},{28,16},{17,29},{21,25},{25,21},{29,17},{1... | collective-permute-start | bytes 294920 | tf_op jit(solution)/shard_map/ppermute | solution.py:276
  405.2 65.6 %collective-permute-start.14 = (bf16[128,384]{1,0:T(8,128)(2,1)S(1)}, bf16[128,384]{1,0:T(8,128)(2,1)S(1)}, u32[]{:S(2)}, u32[]{:S(2)}) collective-permute-start(bf16[128,384]{1,0:T(8,128)(2,1)S(1)} %get-tuple-element.73), channel_id=1, source_target_pairs={{16,24},{20,28},{24,16},{28,20},{17,25},{21,29},{25,17},{29,21},{1... | collective-permute-start | bytes 294920 | tf_op jit(solution)/shard_map/ppermute | solution.py:276
  (60 other events, 740.9 us)

commit v2 on v0

v2 whole, which is shorter than its diff:
```python
import jax
import jax.numpy as jnp
from jax import lax
from jax.experimental import pallas as pl
from jax.experimental.pallas import tpu as pltpu
from jax.sharding import PartitionSpec as P

SHARES = (1, 2, 1)
LIMIT = 40 * 1024 * 1024
LOW = jnp.bfloat16
F32 = jnp.float32


def gelu_slope(pre):
    normal_cdf = 0.5 * (1.0 + jax.scipy.special.erf(pre * 0.7071067811865476))
    density = jnp.exp(-0.5 * pre * pre) * 0.3989422804014327
    return normal_cdf + pre * density


def params():
    return pltpu.CompilerParams(
        vmem_limit_bytes=LIMIT, dimension_semantics=("arbitrary",)
    )


def divisor(size, most):
    return max(r for r in range(16, most + 1, 16) if size % r == 0)


def product(scalars, mat, block, place, steps, right, kinds, base=None):
    depth, tokens = right.shape
    rows = block[0]

    def body(s, mat_ref, right_ref, *refs):
        @pl.when(s[0] == 1)
        def _():
            got = jnp.dot(mat_ref[...], right_ref[...], preferred_element_type=F32)
            outs = refs
            if base is not None:
                got = got + refs[0][...].astype(F32)
                outs = refs[1:]
            for ref in outs:
                ref[...] = got.astype(ref.dtype)

    spec = pl.BlockSpec((rows, tokens), lambda i, s: (i * s[0], 0))
    return pl.pallas_call(
        body,
        grid_spec=pltpu.PrefetchScalarGridSpec(
            num_scalar_prefetch=1,
            grid=(steps,),
            in_specs=[
                pl.BlockSpec(block, lambda i, s: place(i * s[0], s[1] * s[0], s[0])),
                pl.BlockSpec((depth, tokens), lambda i, s: (0, 0)),
            ]
            + [spec] * (base is not None),
            out_specs=[spec] * len(kinds),
        ),
        out_shape=[jax.ShapeDtypeStruct((rows * steps, tokens), kind) for kind in kinds],
        compiler_params=params(),
        cost_estimate=pl.CostEstimate(
            flops=2 * tokens * block[0] * block[1] * steps,
            bytes_accessed=2 * block[0] * block[1] * steps,
            transcendentals=0,
        ),
    )(scalars, mat, right, *([] if base is None else [base]))


def split_rows(scalars, mat):
    rows, cols = mat.shape
    step = 256
    half = step // 2
    group = 2

    def body(s, mat_ref, out_ref):
        @pl.when(s[0] == 1)
        def _():
            to = lax.broadcasted_iota(jnp.int32, (step, step), 0)
            source = lax.broadcasted_iota(jnp.int32, (step, step), 1)
            wanted = jnp.where(to < half, 2 * to, 2 * (to - half) + 1)
            pick = jnp.where(source == wanted, 1.0, 0.0).astype(LOW)
            for g in range(group):
                block = mat_ref[g * step : (g + 1) * step]
                got = jnp.dot(pick, block, preferred_element_type=F32).astype(LOW)
                out_ref[0, g * half : (g + 1) * half] = got[:half]
                out_ref[1, g * half : (g + 1) * half] = got[half:]

    out = pl.pallas_call(
        body,
        grid_spec=pltpu.PrefetchScalarGridSpec(
            num_scalar_prefetch=1,
            grid=(rows // (group * step),),
            in_specs=[pl.BlockSpec((group * step, cols), lambda i, s: (i * s[0], 0))],
            out_specs=pl.BlockSpec((2, group * half, cols), lambda i, s: (0, i * s[0], 0)),
        ),
        out_shape=jax.ShapeDtypeStruct((2, rows // 2, cols), LOW),
        compiler_params=params(),
        cost_estimate=pl.CostEstimate(
            flops=2 * rows * step * cols, bytes_accessed=4 * rows * cols, transcendentals=0
        ),
    )(scalars, mat)
    return out.reshape(rows, cols)


def finish(scalars, out, between, start, total_tokens, term):
    columns, tokens = between.shape
    lanes = 128

    def body(s, *refs):
        between_ref, term_ref = refs[1:3] if out is not None else refs[:2]
        out_ref = refs[-1]
        source = lax.broadcasted_iota(jnp.int32, (2 * lanes, 2 * lanes), 1)
        to = lax.broadcasted_iota(jnp.int32, (2 * lanes, 2 * lanes), 0)
        wanted = jnp.where(source < lanes, 2 * source, 2 * (source - lanes) + 1)
        pick = jnp.where(to == wanted, 1.0, 0.0).astype(LOW)

        @pl.when(s[0] == 0)
        def _():
            out_ref[...] = between_ref[...].T

        @pl.when(s[0] == 1)
        def _():
            for group in range(columns // (2 * lanes)):
                odd_at = columns // 2 + group * lanes
                even = term_ref[group * lanes : (group + 1) * lanes]
                odd = term_ref[odd_at : odd_at + lanes]
                pair = jnp.concatenate([even, odd], axis=0)
                woven = jnp.dot(pick, pair, preferred_element_type=F32)
                at = slice(group * 2 * lanes, (group + 1) * 2 * lanes)
                out_ref[:, at] = (between_ref[at] + woven).T

    earlier = [] if out is None else [out]
    block = pl.BlockSpec((columns, lanes), lambda i, s: (0, i))
    return pl.pallas_call(
        body,
        grid_spec=pltpu.PrefetchScalarGridSpec(
            num_scalar_prefetch=1,
            grid=(tokens // lanes,),
            in_specs=[pl.BlockSpec(memory_space=pl.ANY)] * len(earlier) + [block, block],
            out_specs=pl.BlockSpec((lanes, columns), lambda i, s: (start // lanes + i, 0)),
        ),
        out_shape=jax.ShapeDtypeStruct((total_tokens, columns), F32),
        input_output_aliases={1: 0} if earlier else {},
        compiler_params=params(),
    )(scalars, *earlier, between, term)


def local(grad_out, weight_in, weight_out, pre_act):
    hids = lax.axis_size("hid")
    section = lax.axis_index("section")
    side = lax.axis_index("wid") % 2
    is_up = section == 1

    def scalars(active_section):
        active = (section == active_section).astype(jnp.int32)
        return jnp.stack([active, side]).astype(jnp.int32)

    down, up = scalars(0), scalars(1)

    def within(active, distance, block):
        size = lax.axis_size("wid")
        pairs = [(active * size + i, active * size + (i ^ distance)) for i in range(size)]
        return lax.ppermute(block, ("section", "wid"), pairs)

    mat_in = weight_in[0]
    mat_out = weight_out[0]
    quarter, hid_tile = mat_in.shape
    half = hid_tile // 2
    batches, batch_tokens, _ = grad_out.shape
    total = batches * batch_tokens
    unit = total // sum(SHARES)
    starts = [unit * sum(SHARES[:k]) for k in range(len(SHARES))]
    sizes = [unit * share for share in SHARES]
    chunks = range(len(SHARES))
    grad = grad_out.reshape(total, quarter)
    pre = pre_act[0].reshape(total, hid_tile)

    split_out = split_rows(up, mat_out)

    def slope_of(k):
        own = lax.dynamic_slice(pre, (starts[k], side * half), (sizes[k], half))
        return lax.optimization_barrier(gelu_slope(own).T)

    slopes = [slope_of(k) for k in chunks]
    grads = [grad[starts[k] : starts[k] + sizes[k]].T for k in chunks]

    hid_rows = divisor(half, 1024)
    hid_steps = half // hid_rows
    hid_block = (hid_rows, quarter)
    width_rows = divisor(quarter, 512)
    pair_rows = divisor(quarter // 2, 512)
    pair_steps = quarter // 2 // pair_rows

    def reduce_hid(partial):
        parts = partial.reshape(hids, quarter // hids, partial.shape[1])
        got = lax.all_to_all(parts, "hid", 0, 0)
        return got.astype(F32).sum(0).astype(LOW)

    def gather_hid(term):
        got = lax.all_gather(term, "hid", axis=0)
        return got.reshape(quarter, term.shape[1])

    def backward(k, active, hidden_grad, low_grad):
        other = within(active, 2, low_grad)
        return ((hidden_grad + other.astype(F32)) * slopes[k]).astype(LOW)

    def down_chunk(k, flags):
        low = grads[k].astype(LOW)
        (sent,) = product(
            flags, mat_out, hid_block, lambda i, b, on: ((on - b) * hid_steps + i, 0),
            hid_steps, low, (LOW,),
        )
        got = within(0, 1, sent)
        full, low_grad = product(
            flags, mat_out, hid_block, lambda i, b, on: (b * hid_steps + i, 0),
            hid_steps, low, (F32, LOW), got,
        )
        hidden = backward(k, 0, full, low_grad)
        swapped = within(0, 1, hidden)
        (partial,) = product(
            down, mat_in, (width_rows, half), lambda i, b, on: (i, b),
            quarter // width_rows, hidden, (F32,),
        )
        (partial,) = product(
            down, mat_in, (width_rows, half), lambda i, b, on: (i, on - b),
            quarter // width_rows, swapped, (LOW,), partial,
        )
        term = reduce_hid(partial)
        crossed = lax.ppermute(term, "section", [(0, 1)])
        term = gather_hid(jnp.where(is_up, crossed, term))
        return grads[k] + term.astype(F32), low_grad

    def up_chunk(k, out, between):
        low = between.astype(LOW)
        low_other = within(1, 1, low)
        (partial,) = product(
            up, split_out, hid_block, lambda i, b, on: (b * hid_steps + i, 0),
            hid_steps, low, (F32,),
        )
        full, low_grad = product(
            up, split_out, hid_block, lambda i, b, on: ((on - b) * hid_steps + i, 0),
            hid_steps, low_other, (F32, LOW), partial,
        )
        hidden = backward(k, 1, full, low_grad)

        def place(i, core):
            return core * pair_steps + i % pair_steps, i // pair_steps

        (sent,) = product(
            up, mat_in, (pair_rows, half), lambda i, b, on: place(i, on - b),
            2 * pair_steps, hidden, (F32,),
        )
        got = within(1, 1, sent)
        (partial,) = product(
            up, mat_in, (pair_rows, half), lambda i, b, on: place(i, b),
            2 * pair_steps, hidden, (LOW,), got,
        )
        term = gather_hid(reduce_hid(partial))
        return finish(up, out, between, starts[k], total, term)

    firsts = []
    flags = down
    for k in chunks:
        between, last = down_chunk(k, flags)
        firsts.append(between)
        flags, _ = lax.optimization_barrier((down, last))
    out = None
    for k in chunks:
        out = up_chunk(k, out, firsts[k])
    return out.reshape(1, batches, batch_tokens, quarter)


def solution(mesh):
    return jax.shard_map(
        local,
        mesh=mesh,
        in_specs=(
            P(None, None, "wid"),
            P("section", "wid", "hid"),
            P("section", "hid", "wid"),
            P("section", None, None, "hid"),
        ),
        out_specs=P("section", None, None, "wid"),
        check_vma=False,
    )
```

time: 852 us -> 443 us (0.52)
  waiting for transfers between devices: 593 us -> 64.8 us
  Pallas kernels: 0 us -> 143 us
  blocking collectives: 0 us -> 117 us
  other arithmetic: 93.2 us -> 24.5 us
  matrix products: 68.1 us -> 0 us
  starting transfers between devices: 3.46 us -> 58.4 us
  local copies, waits for them, and re-layouts: 77.4 us -> 31.6 us
  between operations: 13.8 us -> 0.63 us
    psum x6 -> x0, waiting for transfers between devices: 508 us -> none  [the longest x3 299 us: local(): hidden_grad = lax.psum(partial_hidden, 'wid')]
    pallas_call x0 -> x28, Pallas kernels: none -> 143 us  [the longest x24 117 us: product(): pl.pallas_call(body, grid_spec=pltpu.PrefetchScalarGridSpec(num_scalar_pr...]
    all_gather x0 -> x6, blocking collectives: none -> 117 us  [gather_hid(): got = lax.all_gather(term, 'hid', axis=0)]
    dot_general x12 -> x0, matrix products: 68.1 us -> none  [the longest x3 21.4 us: local(): lax.dot_general(second_in, out_high, contract, preferred_element_type=jnp...]
    select_n x5 -> x3, other arithmetic: 56 us -> 1.61 us  [down_chunk(): term = gather_hid(jnp.where(is_up, crossed, term))]
    slice x3 -> x2, local copies, waits for them, and re-layouts: 41.6 us -> 3.61 us  [local(): grads = [grad[starts[k]:starts[k] + sizes[k]].T for k in chunks]]
    ppermute x7 -> x21, waiting for transfers between devices: 85.8 us -> 50 us  [the longest x3 42 us: down_chunk(): crossed = lax.ppermute(term, 'section', [(0, 1)])]
    ppermute x7 -> x21, starting transfers between devices: 3.25 us -> 33 us  [the longest x18 29 us: within(): return lax.ppermute(block, ('section', 'wid'), pairs)]
  transfers between devices with their start and end apart: 13 -> 27, of which waited for: 13 -> 7; matrix products, arithmetic and copies ran while one was open for 7% -> 11% of each run, Pallas kernels for 0% -> 29%
where the time goes in v2:
time: 443 us; the launch traced here: 440 us
  Pallas kernels  143 us (32%)
  blocking collectives  117 us (26%)
  waiting for transfers between devices  64.8 us (15%)
  starting transfers between devices  58.4 us (13%)
  local copies, waits for them, and re-layouts  31.6 us (7%)
  other arithmetic  24.5 us (6%)
    all_gather x6, blocking collectives, gather_hid(): got = lax.all_gather(term, 'hid', axis=0)  117 us
    pallas_call x24, Pallas kernels, product(): pl.pallas_call(body, grid_spec=pltpu.PrefetchScalarGridSpec(num_scalar_pr...  117 us
    ppermute x3, waiting for transfers between devices, down_chunk(): crossed = lax.ppermute(term, 'section', [(0, 1)])  42 us
    ppermute x18, starting transfers between devices, within(): return lax.ppermute(block, ('section', 'wid'), pairs)  29 us
    all_to_all x6, starting transfers between devices, reduce_hid(): got = lax.all_to_all(parts, 'hid', 0, 0)  25.5 us
    unnamed x50, local copies, waits for them, and re-layouts  20.3 us
    pallas_call x1, Pallas kernels, split_rows(): pl.pallas_call(body, grid_spec=pltpu.PrefetchScalarGridSpec(num_scalar_pr...  20 us
    all_to_all x6, waiting for transfers between devices, reduce_hid(): got = lax.all_to_all(parts, 'hid', 0, 0)  14.8 us
  transfers between devices with their start and end apart: 27, of which 7 were waited for; matrix products, arithmetic and copies ran while one was open for 11% of the time, Pallas kernels for 29%

profile of v2, /device:TPU:2, one launch (start us, length us, event | category | flops | bytes accessed | tf_op | source)
XLA Modules:
  0.0 440.2 jit_solution(16386222258305374132)
XLA Ops:
  74.1 5.6 %all-to-all-done = bf16[4,384,128]{2,1,0:T(8,128)(2,1)} async-done(((bf16[4,384,128]{2,1,0:T(8,128)(2,1)}), bf16[4,384,128]{2,1,0:T(8,128)(2,1)}, u32[]{:S(2)}, u32[]{:S(2)}) %all-to-all-start) | async-done | bytes 393248 | tf_op jit(solution)/shard_map/all_to_all | solution.py:195
  88.8 20.0 %shard_map.50 = bf16[2,3072,1536]{2,1,0:T(8,128)(2,1)} custom-call(s32[2]{0:T(128)S(1)} %pad_add_fusion.s, bf16[6144,1536]{1,0:T(8,128)(2,1)} %bitcast.51), custom_call_target="tpu_custom_call" | custom-call | flops 4831838208 | bytes 37748736 | tf_op jit(solution)/shard_map/pallas_call | solution.py:87
  108.8 19.7 %collective-permute-done.3 = bf16[384,128]{1,0:T(8,128)(2,1)S(1)} collective-permute-done((bf16[384,128]{1,0:T(8,128)(2,1)}, bf16[384,128]{1,0:T(8,128)(2,1)S(1)}, u32[]{:S(2)}, u32[]{:S(2)}) %collective-permute-start.3) | collective-permute-done | bytes 98336 | tf_op jit(solution)/shard_map/ppermute | solution.py:228
  141.8 25.2 %all-gather = bf16[1536,128]{1,0:T(8,128)(2,1)S(1)} all-gather(bf16[384,128]{1,0:T(8,128)(2,1)S(1)} %copy-done.21), channel_id=2, replica_groups=mesh['section'=2,'hid'=4,'wid'=4] {'hid'}, dimensions={0}, use_global_device_ids=true | all-gather | bytes 491520 | tf_op jit(solution)/shard_map/all_gather | solution.py:199
  183.0 13.1 %collective-permute-done.10 = bf16[384,256]{1,0:T(8,128)(2,1)} collective-permute-done((bf16[384,256]{1,0:T(8,128)(2,1)}, bf16[384,256]{1,0:T(8,128)(2,1)}, u32[]{:S(2)}, u32[]{:S(2)}) %collective-permute-start.10) | collective-permute-done | bytes 196640 | tf_op jit(solution)/shard_map/ppermute | solution.py:228
  197.1 17.8 %all-gather.2 = bf16[1536,256]{1,0:T(8,128)(2,1)S(1)} all-gather(bf16[384,256]{1,0:T(8,128)(2,1)S(1)} %broadcast_select_fusion), channel_id=4, replica_groups=mesh['section'=2,'hid'=4,'wid'=4] {'hid'}, dimensions={0}, use_global_device_ids=true | all-gather | bytes 983040 | tf_op jit(solution)/shard_map/all_gather | solution.py:199
  218.2 6.3 %shard_map.51.refs_0_ = f32[3072,128]{1,0:T(8,128)S(1)} custom-call(s32[2]{0:T(128)S(1)} %pad_add_fusion.s, bf16[6144,1536]{1,0:T(8,128)(2,1)} %bitcast.52, bf16[1536,128]{1,0:T(8,128)(2,1)S(1)} %get-tuple-element.37.right_ref), custom_call_target="tpu_custom_call" | custom-call | flops 1207959552 | bytes 9437184 | tf_op jit(solution)/shard_map/pallas_call | solution.py:46
  227.7 6.4 %shard_map.52 = (f32[3072,128]{1,0:T(8,128)S(1)}, bf16[3072,128]{1,0:T(8,128)(2,1)S(1)}) custom-call(s32[2]{0:T(128)S(1)} %pad_add_fusion.s, bf16[6144,1536]{1,0:T(8,128)(2,1)} %bitcast.53, bf16[1536,128]{1,0:T(8,128)(2,1)} %collective-permute-done.4.right_ref, f32[3072,128]{1,0:T(8,128)S(1)} %shard_map.51.refs_0_), custom_call_target="tpu_custom_call" | custom-call | flops 1207959552 | bytes 9437184 | tf_op jit(solution)/shard_map/pallas_call | solution.py:46
  236.5 9.2 %collective-permute-done.17 = bf16[384,128]{1,0:T(8,128)(2,1)S(1)} collective-permute-done((bf16[384,128]{1,0:T(8,128)(2,1)}, bf16[384,128]{1,0:T(8,128)(2,1)S(1)}, u32[]{:S(2)}, u32[]{:S(2)}) %collective-permute-start.17) | collective-permute-done | bytes 98336 | tf_op jit(solution)/shard_map/ppermute | solution.py:228
  245.8 14.4 %all-gather.4 = bf16[1536,128]{1,0:T(8,128)(2,1)S(1)} all-gather(bf16[384,128]{1,0:T(8,128)(2,1)S(1)} %broadcast_select_fusion.1), channel_id=6, replica_groups=mesh['section'=2,'hid'=4,'wid'=4] {'hid'}, dimensions={0}, use_global_device_ids=true | all-gather | bytes 491520 | tf_op jit(solution)/shard_map/all_gather | solution.py:199
  260.1 6.3 %shard_map.60.refs_0_ = f32[3072,256]{1,0:T(8,128)S(1)} custom-call(s32[2]{0:T(128)S(1)} %pad_add_fusion.s, bf16[6144,1536]{1,0:T(8,128)(2,1)} %bitcast.54, bf16[1536,256]{1,0:T(8,128)(2,1)S(1)} %get-tuple-element.35.right_ref), custom_call_target="tpu_custom_call" | custom-call | flops 2415919104 | bytes 9437184 | tf_op jit(solution)/shard_map/pallas_call | solution.py:46
  266.5 6.5 %shard_map.61 = (f32[3072,256]{1,0:T(8,128)S(1)}, bf16[3072,256]{1,0:T(8,128)(2,1)S(1)}) custom-call(s32[2]{0:T(128)S(1)} %pad_add_fusion.s, bf16[6144,1536]{1,0:T(8,128)(2,1)} %bitcast.55, bf16[1536,256]{1,0:T(8,128)(2,1)} %collective-permute-done.11.right_ref, f32[3072,256]{1,0:T(8,128)S(1)} %shard_map.60.refs_0_), custom_call_target="tpu_custom_call" | custom-call | flops 2415919104 | bytes 9437184 | tf_op jit(solution)/shard_map/pallas_call | solution.py:46
  278.7 6.5 %shard_map.53 = f32[1536,128]{1,0:T(8,128)S(1)} custom-call(s32[2]{0:T(128)S(1)} %pad_add_fusion.s, bf16[1536,6144]{1,0:T(8,128)(2,1)} %bitcast.39, bf16[3072,128]{1,0:T(8,128)(2,1)S(1)} %multiply_convert_fusion.4.right_ref), custom_call_target="tpu_custom_call" | custom-call | flops 1207959552 | bytes 9437184 | tf_op jit(solution)/shard_map/pallas_call | solution.py:46
  287.6 6.3 %shard_map.69.refs_0_ = f32[3072,128]{1,0:T(8,128)S(1)} custom-call(s32[2]{0:T(128)S(1)} %pad_add_fusion.s, bf16[6144,1536]{1,0:T(8,128)(2,1)} %bitcast.56, bf16[1536,128]{1,0:T(8,128)(2,1)S(1)} %get-tuple-element.33.right_ref), custom_call_target="tpu_custom_call" | custom-call | flops 1207959552 | bytes 9437184 | tf_op jit(solution)/shard_map/pallas_call | solution.py:46
  294.0 6.6 %shard_map.70 = (f32[3072,128]{1,0:T(8,128)S(1)}, bf16[3072,128]{1,0:T(8,128)(2,1)S(1)}) custom-call(s32[2]{0:T(128)S(1)} %pad_add_fusion.s, bf16[6144,1536]{1,0:T(8,128)(2,1)} %bitcast.57, bf16[1536,128]{1,0:T(8,128)(2,1)S(1)} %collective-permute-done.18.right_ref, f32[3072,128]{1,0:T(8,128)S(1)} %shard_map.69.refs_0_), custom_call_target="tpu_custom_call" | custom-call | flops 1207959552 | bytes 9437184 | tf_op jit(solution)/shard_map/pallas_call | solution.py:46
  304.6 7.4 %shard_map.62 = f32[1536,256]{1,0:T(8,128)} custom-call(s32[2]{0:T(128)S(1)} %pad_add_fusion.s, bf16[1536,6144]{1,0:T(8,128)(2,1)} %bitcast.40, bf16[3072,256]{1,0:T(8,128)(2,1)S(1)} %multiply_convert_fusion.right_ref), custom_call_target="tpu_custom_call" | custom-call | flops 2415919104 | bytes 9437184 | tf_op jit(solution)/shard_map/pallas_call | solution.py:46
  313.9 8.0 %collective-permute-done.19 = bf16[3072,128]{1,0:T(8,128)(2,1)S(1)} collective-permute-done((bf16[3072,128]{1,0:T(8,128)(2,1)S(1)}, bf16[3072,128]{1,0:T(8,128)(2,1)S(1)}, u32[]{:S(2)}, u32[]{:S(2)}) %collective-permute-start.19) | collective-permute-done | bytes 786464 | tf_op jit(solution)/shard_map/ppermute | solution.py:162
  322.1 7.2 %shard_map.71 = f32[1536,128]{1,0:T(8,128)} custom-call(s32[2]{0:T(128)S(1)} %pad_add_fusion.s, bf16[1536,6144]{1,0:T(8,128)(2,1)} %bitcast.41, bf16[3072,128]{1,0:T(8,128)(2,1)S(1)} %multiply_convert_fusion.2.right_ref), custom_call_target="tpu_custom_call" | custom-call | flops 1207959552 | bytes 9437184 | tf_op jit(solution)/shard_map/pallas_call | solution.py:46
  331.5 7.2 %shard_map.54 = bf16[1536,128]{1,0:T(8,128)(2,1)} custom-call(s32[2]{0:T(128)S(1)} %pad_add_fusion.s, bf16[1536,6144]{1,0:T(8,128)(2,1)} %bitcast.42, bf16[3072,128]{1,0:T(8,128)(2,1)S(1)} %multiply_convert_fusion.4.right_ref, f32[1536,128]{1,0:T(8,128)S(1)} %collective-permute-done.6.refs_0_), custom_call_target="tpu_custom_call" | custom-call | flops 1207959552 | bytes 9437184 | tf_op jit(solution)/shard_map/pallas_call | solution.py:46
  342.9 7.2 %shard_map.72 = bf16[1536,128]{1,0:T(8,128)(2,1)} custom-call(s32[2]{0:T(128)S(1)} %pad_add_fusion.s, bf16[1536,6144]{1,0:T(8,128)(2,1)} %bitcast.43, bf16[3072,128]{1,0:T(8,128)(2,1)S(1)} %multiply_convert_fusion.2.right_ref, f32[1536,128]{1,0:T(8,128)} %collective-permute-done.20.refs_0_), custom_call_target="tpu_custom_call" | custom-call | flops 1207959552 | bytes 9437184 | tf_op jit(solution)/shard_map/pallas_call | solution.py:46
  358.7 7.4 %shard_map.63 = bf16[1536,256]{1,0:T(8,128)(2,1)} custom-call(s32[2]{0:T(128)S(1)} %pad_add_fusion.s, bf16[1536,6144]{1,0:T(8,128)(2,1)} %bitcast.44, bf16[3072,256]{1,0:T(8,128)(2,1)S(1)} %multiply_convert_fusion.right_ref, f32[1536,256]{1,0:T(8,128)} %collective-permute-done.13.refs_0_), custom_call_target="tpu_custom_call" | custom-call | flops 2415919104 | bytes 9437184 | tf_op jit(solution)/shard_map/pallas_call | solution.py:46
  373.8 26.6 %all-gather.1.refs_1_ = bf16[1536,128]{1,0:T(8,128)(2,1)S(1)} all-gather(bf16[384,128]{1,0:T(8,128)(2,1)S(1)} %reduce_sum.73), channel_id=3, replica_groups=mesh['section'=2,'hid'=4,'wid'=4] {'hid'}, dimensions={0}, use_global_device_ids=true | all-gather | bytes 491520 | tf_op jit(solution)/shard_map/all_gather | solution.py:199
  402.4 15.6 %all-gather.5.refs_2_ = bf16[1536,128]{1,0:T(8,128)(2,1)S(1)} all-gather(bf16[384,128]{1,0:T(8,128)(2,1)S(1)} %reduce_sum.77), channel_id=7, replica_groups=mesh['section'=2,'hid'=4,'wid'=4] {'hid'}, dimensions={0}, use_global_device_ids=true | all-gather | bytes 491520 | tf_op jit(solution)/shard_map/all_gather | solution.py:199
  418.2 17.5 %all-gather.3.refs_2_ = bf16[1536,256]{1,0:T(8,128)(2,1)S(1)} all-gather(bf16[384,256]{1,0:T(8,128)(2,1)S(1)} %reduce_sum.75), channel_id=5, replica_groups=mesh['section'=2,'hid'=4,'wid'=4] {'hid'}, dimensions={0}, use_global_device_ids=true | all-gather | bytes 983040 | tf_op jit(solution)/shard_map/all_gather | solution.py:199
  (144 shorter events, 165.6 us)
Async XLA Ops:
  6.3 13.9 %collective-permute-start = (bf16[3072,128]{1,0:T(8,128)(2,1)S(1)}, bf16[3072,128]{1,0:T(8,128)(2,1)S(1)}, u32[]{:S(2)}, u32[]{:S(2)}) collective-permute-start(bf16[3072,128]{1,0:T(8,128)(2,1)S(1)} %shard_map.46), channel_id=1, source_target_pairs={{0,1},{1,0},{2,3},{3,2},{4,5},{5,4},{6,7},{7,6},{8,9},{9,8},{10,11... | collective-permute-start | bytes 2359304 | tf_op jit(solution)/shard_map/ppermute | solution.py:162
  27.4 18.0 %collective-permute-start.7 = (bf16[3072,256]{1,0:T(8,128)(2,1)}, bf16[3072,256]{1,0:T(8,128)(2,1)S(1)}, u32[]{:S(2)}, u32[]{:S(2)}) collective-permute-start(bf16[3072,256]{1,0:T(8,128)(2,1)} %shard_map.56), channel_id=1, source_target_pairs={{0,1},{1,0},{2,3},{3,2},{4,5},{5,4},{6,7},{7,6},{8,9},{9,8},{10,11... | collective-permute-start | bytes 4718600 | tf_op jit(solution)/shard_map/ppermute | solution.py:162
  50.8 17.1 %collective-permute-start.8 = (bf16[3072,256]{1,0:T(8,128)(2,1)}, bf16[3072,256]{1,0:T(8,128)(2,1)S(1)}, u32[]{:S(2)}, u32[]{:S(2)}) collective-permute-start(bf16[3072,256]{1,0:T(8,128)(2,1)} %get-tuple-element.25), channel_id=1, source_target_pairs={{0,2},{1,3},{2,0},{3,1},{4,6},{5,7},{6,4},{7,5},{8,10},{9,11},{10,... | collective-permute-start | bytes 4718600 | tf_op jit(solution)/shard_map/ppermute | solution.py:162
  58.3 24.4 %collective-permute-start.14 = (bf16[3072,128]{1,0:T(8,128)(2,1)}, bf16[3072,128]{1,0:T(8,128)(2,1)}, u32[]{:S(2)}, u32[]{:S(2)}) collective-permute-start(bf16[3072,128]{1,0:T(8,128)(2,1)} %shard_map.65), channel_id=1, source_target_pairs={{0,1},{1,0},{2,3},{3,2},{4,5},{5,4},{6,7},{7,6},{8,9},{9,8},{10,11... | collective-permute-start | bytes 2359304 | tf_op jit(solution)/shard_map/ppermute | solution.py:162
  63.0 16.7 %all-to-all-start = ((bf16[4,384,128]{2,1,0:T(8,128)(2,1)}), bf16[4,384,128]{2,1,0:T(8,128)(2,1)}, u32[]{:S(2)}, u32[]{:S(2)}) async-start(bf16[4,384,128]{2,1,0:T(8,128)(2,1)} %bitcast.9), calls=%async_computation | async-start | bytes 786432 | tf_op jit(solution)/shard_map/all_to_all | solution.py:195
  71.6 60.0 %collective-permute-start.9 = (bf16[3072,256]{1,0:T(8,128)(2,1)S(1)}, bf16[3072,256]{1,0:T(8,128)(2,1)S(1)}, u32[]{:S(2)}, u32[]{:S(2)}) collective-permute-start(bf16[3072,256]{1,0:T(8,128)(2,1)S(1)} %multiply_convert_fusion.1.right_ref), channel_id=1, source_target_pairs={{0,1},{1,0},{2,3},{3,2},{4,5},{5,4},{6,7},{7,6},{8,9},{9,8},{10,11... | collective-permute-start | bytes 4718600 | tf_op jit(solution)/shard_map/ppermute | solution.py:162
  81.4 47.1 %collective-permute-start.3 = (bf16[384,128]{1,0:T(8,128)(2,1)}, bf16[384,128]{1,0:T(8,128)(2,1)S(1)}, u32[]{:S(2)}, u32[]{:S(2)}) collective-permute-start(bf16[384,128]{1,0:T(8,128)(2,1)} %reduce_sum.72), channel_id=1, source_target_pairs={{0,16},{1,17},{2,18},{3,19},{4,20},{5,21},{6,22},{7,23},{8,24},{9,... | collective-permute-start | bytes 294920 | tf_op jit(solution)/shard_map/ppermute | solution.py:228
  87.1 52.0 %collective-permute-start.15 = (bf16[3072,128]{1,0:T(8,128)(2,1)}, bf16[3072,128]{1,0:T(8,128)(2,1)}, u32[]{:S(2)}, u32[]{:S(2)}) collective-permute-start(bf16[3072,128]{1,0:T(8,128)(2,1)} %get-tuple-element.30), channel_id=1, source_target_pairs={{0,2},{1,3},{2,0},{3,1},{4,6},{5,7},{6,4},{7,5},{8,10},{9,11},{10,... | collective-permute-start | bytes 2359304 | tf_op jit(solution)/shard_map/ppermute | solution.py:162
  134.7 34.4 %all-to-all-start.2 = ((bf16[4,384,256]{2,1,0:T(8,128)(2,1)}), bf16[4,384,256]{2,1,0:T(8,128)(2,1)}, u32[]{:S(2)}, u32[]{:S(2)}) async-start(bf16[4,384,256]{2,1,0:T(8,128)(2,1)} %bitcast.14), calls=%async_computation.2 | async-start | bytes 1572864 | tf_op jit(solution)/shard_map/all_to_all | solution.py:195
  141.1 33.7 %collective-permute-start.16 = (bf16[3072,128]{1,0:T(8,128)(2,1)S(1)}, bf16[3072,128]{1,0:T(8,128)(2,1)S(1)}, u32[]{:S(2)}, u32[]{:S(2)}) collective-permute-start(bf16[3072,128]{1,0:T(8,128)(2,1)S(1)} %multiply_convert_fusion.3.right_ref), channel_id=1, source_target_pairs={{0,1},{1,0},{2,3},{3,2},{4,5},{5,4},{6,7},{7,6},{8,9},{9,8},{10,11... | collective-permute-start | bytes 2359304 | tf_op jit(solution)/shard_map/ppermute | solution.py:162
  167.2 60.5 %collective-permute-start.4 = (bf16[1536,128]{1,0:T(8,128)(2,1)S(1)}, bf16[1536,128]{1,0:T(8,128)(2,1)}, u32[]{:S(2)}, u32[]{:S(2)}) collective-permute-start(bf16[1536,128]{1,0:T(8,128)(2,1)S(1)} %get-tuple-element.37.right_ref), channel_id=1, source_target_pairs={{16,17},{17,16},{18,19},{19,18},{20,21},{21,20},{22,23},{23,22},{2... | collective-permute-start | bytes 1179656 | tf_op jit(solution)/shard_map/ppermute | solution.py:162
  171.1 25.0 %collective-permute-start.10 = (bf16[384,256]{1,0:T(8,128)(2,1)}, bf16[384,256]{1,0:T(8,128)(2,1)}, u32[]{:S(2)}, u32[]{:S(2)}) collective-permute-start(bf16[384,256]{1,0:T(8,128)(2,1)} %reduce_sum.74), channel_id=1, source_target_pairs={{0,16},{1,17},{2,18},{3,19},{4,20},{5,21},{6,22},{7,23},{8,24},{9,... | collective-permute-start | bytes 589832 | tf_op jit(solution)/shard_map/ppermute | solution.py:228
  177.9 46.6 %all-to-all-start.4 = ((bf16[4,384,128]{2,1,0:T(8,128)(2,1)}), bf16[4,384,128]{2,1,0:T(8,128)(2,1)}, u32[]{:S(2)}, u32[]{:S(2)}) async-start(bf16[4,384,128]{2,1,0:T(8,128)(2,1)} %bitcast.18), calls=%async_computation.4 | async-start | bytes 786432 | tf_op jit(solution)/shard_map/all_to_all | solution.py:195
  216.3 50.2 %collective-permute-start.11 = (bf16[1536,256]{1,0:T(8,128)(2,1)S(1)}, bf16[1536,256]{1,0:T(8,128)(2,1)}, u32[]{:S(2)}, u32[]{:S(2)}) collective-permute-start(bf16[1536,256]{1,0:T(8,128)(2,1)S(1)} %get-tuple-element.35.right_ref), channel_id=1, source_target_pairs={{16,17},{17,16},{18,19},{19,18},{20,21},{21,20},{22,23},{23,22},{2... | collective-permute-start | bytes 2359304 | tf_op jit(solution)/shard_map/ppermute | solution.py:162
  226.2 19.5 %collective-permute-start.17 = (bf16[384,128]{1,0:T(8,128)(2,1)}, bf16[384,128]{1,0:T(8,128)(2,1)S(1)}, u32[]{:S(2)}, u32[]{:S(2)}) collective-permute-start(bf16[384,128]{1,0:T(8,128)(2,1)} %reduce_sum.76), channel_id=1, source_target_pairs={{0,16},{1,17},{2,18},{3,19},{4,20},{5,21},{6,22},{7,23},{8,24},{9,... | collective-permute-start | bytes 294920 | tf_op jit(solution)/shard_map/ppermute | solution.py:228
  234.1 44.4 %collective-permute-start.5 = (bf16[3072,128]{1,0:T(8,128)(2,1)S(1)}, bf16[3072,128]{1,0:T(8,128)(2,1)S(1)}, u32[]{:S(2)}, u32[]{:S(2)}) collective-permute-start(bf16[3072,128]{1,0:T(8,128)(2,1)S(1)} %get-tuple-element.22), channel_id=1, source_target_pairs={{16,18},{17,19},{18,16},{19,17},{20,22},{21,23},{22,20},{23,21},{2... | collective-permute-start | bytes 2359304 | tf_op jit(solution)/shard_map/ppermute | solution.py:162
  273.0 31.0 %collective-permute-start.12 = (bf16[3072,256]{1,0:T(8,128)(2,1)S(1)}, bf16[3072,256]{1,0:T(8,128)(2,1)S(1)}, u32[]{:S(2)}, u32[]{:S(2)}) collective-permute-start(bf16[3072,256]{1,0:T(8,128)(2,1)S(1)} %get-tuple-element.27), channel_id=1, source_target_pairs={{16,18},{17,19},{18,16},{19,17},{20,22},{21,23},{22,20},{23,21},{2... | collective-permute-start | bytes 4718600 | tf_op jit(solution)/shard_map/ppermute | solution.py:162
  276.6 17.4 %collective-permute-start.18 = (bf16[1536,128]{1,0:T(8,128)(2,1)S(1)}, bf16[1536,128]{1,0:T(8,128)(2,1)S(1)}, u32[]{:S(2)}, u32[]{:S(2)}) collective-permute-start(bf16[1536,128]{1,0:T(8,128)(2,1)S(1)} %get-tuple-element.33.right_ref), channel_id=1, source_target_pairs={{16,17},{17,16},{18,19},{19,18},{20,21},{21,20},{22,23},{23,22},{2... | collective-permute-start | bytes 1179656 | tf_op jit(solution)/shard_map/ppermute | solution.py:162
  285.2 46.2 %collective-permute-start.6 = (f32[1536,128]{1,0:T(8,128)S(1)}, f32[1536,128]{1,0:T(8,128)S(1)}, u32[]{:S(2)}, u32[]{:S(2)}) collective-permute-start(f32[1536,128]{1,0:T(8,128)S(1)} %shard_map.53), channel_id=1, source_target_pairs={{16,17},{17,16},{18,19},{19,18},{20,21},{21,20},{22,23},{23,22},{2... | collective-permute-start | bytes 2359304 | tf_op jit(solution)/shard_map/ppermute | solution.py:162
  300.6 21.4 %collective-permute-start.19 = (bf16[3072,128]{1,0:T(8,128)(2,1)S(1)}, bf16[3072,128]{1,0:T(8,128)(2,1)S(1)}, u32[]{:S(2)}, u32[]{:S(2)}) collective-permute-start(bf16[3072,128]{1,0:T(8,128)(2,1)S(1)} %get-tuple-element.32), channel_id=1, source_target_pairs={{16,18},{17,19},{18,16},{19,17},{20,22},{21,23},{22,20},{23,21},{2... | collective-permute-start | bytes 2359304 | tf_op jit(solution)/shard_map/ppermute | solution.py:162
  312.0 46.7 %collective-permute-start.13 = (f32[1536,256]{1,0:T(8,128)}, f32[1536,256]{1,0:T(8,128)}, u32[]{:S(2)}, u32[]{:S(2)}) collective-permute-start(f32[1536,256]{1,0:T(8,128)} %shard_map.62), channel_id=1, source_target_pairs={{16,17},{17,16},{18,19},{19,18},{20,21},{21,20},{22,23},{23,22},{2... | collective-permute-start | bytes 4718600 | tf_op jit(solution)/shard_map/ppermute | solution.py:162
  338.6 16.6 %all-to-all-start.1 = ((bf16[4,384,128]{2,1,0:T(8,128)(2,1)}), bf16[4,384,128]{2,1,0:T(8,128)(2,1)S(1)}, u32[]{:S(2)}, u32[]{:S(2)}) async-start(bf16[4,384,128]{2,1,0:T(8,128)(2,1)} %bitcast.11), calls=%async_computation.1 | async-start | bytes 786432 | tf_op jit(solution)/shard_map/all_to_all | solution.py:195
  355.2 15.0 %all-to-all-start.5 = ((bf16[4,384,128]{2,1,0:T(8,128)(2,1)}), bf16[4,384,128]{2,1,0:T(8,128)(2,1)S(1)}, u32[]{:S(2)}, u32[]{:S(2)}) async-start(bf16[4,384,128]{2,1,0:T(8,128)(2,1)} %bitcast.19), calls=%async_computation.5 | async-start | bytes 786432 | tf_op jit(solution)/shard_map/all_to_all | solution.py:195
  370.2 47.8 %all-to-all-start.3 = ((bf16[4,384,256]{2,1,0:T(8,128)(2,1)}), bf16[4,384,256]{2,1,0:T(8,128)(2,1)S(1)}, u32[]{:S(2)}, u32[]{:S(2)}) async-start(bf16[4,384,256]{2,1,0:T(8,128)(2,1)} %bitcast.15), calls=%async_computation.3 | async-start | bytes 1572864 | tf_op jit(solution)/shard_map/all_to_all | solution.py:195
  (25 other events, 271.9 us)

commit v3 on v2

v3 whole, which is shorter than its diff:
```python
import functools

import jax
import jax.numpy as jnp
from jax import lax
from jax.experimental import pallas as pl
from jax.experimental.pallas import tpu as pltpu
from jax.sharding import PartitionSpec as P

SHARES = (1, 2, 1)
PARTS = 4
LANES = 128
LIMIT = 26 * 1024 * 1024
LOW = jnp.bfloat16
F32 = jnp.float32


def gelu_slope(pre):
    normal_cdf = 0.5 * (1.0 + lax.erf(pre * 0.7071067811865476))
    density = jnp.exp(-0.5 * pre * pre) * 0.3989422804014327
    return normal_cdf + pre * density


def params():
    return pltpu.CompilerParams(vmem_limit_bytes=LIMIT)


def divisor(size, most):
    return max(r for r in range(16, most + 1, 16) if size % r == 0)


SMEM = pl.BlockSpec(memory_space=pltpu.SMEM)
VMEM = pl.BlockSpec(memory_space=pltpu.VMEM)
ANY = pl.BlockSpec(memory_space=pl.ANY)


def product(flags, mat, block, place, steps, sources, prepare, tokens, outs, store, base=None):
    rows, depth = block
    slots = min(4, steps)
    bare = prepare is None
    count = len(sources)

    def body(s, mat_ref, *refs):
        source_refs, refs = refs[:count], refs[count:]
        base_ref = None
        if base is not None:
            base_ref, refs = refs[0], refs[1:]
        out_refs, (buf, sem) = refs[:-2], refs[-2:]

        def fetch(i):
            row, col = place(i, s)
            piece = mat_ref.at[pl.ds(pl.multiple_of(row, 16), rows), pl.ds(pl.multiple_of(col, LANES), depth)]
            return pltpu.make_async_copy(piece, buf.at[i % slots], sem.at[i % slots])

        @pl.when(s[0] == 1)
        def _():
            for i in range(slots):
                fetch(i).start()
            right_ref = source_refs[0]
            if not bare:
                right_ref = out_refs[-1]
                prepare(right_ref, *source_refs)
            for i in range(steps):
                fetch(i).wait()
                got = jnp.dot(buf[i % slots], right_ref[...], preferred_element_type=F32)
                if i + slots < steps:
                    fetch(i + slots).start()
                targets, base_row = store(i, s)
                if base_ref is not None:
                    start = pl.multiple_of(base_row, 16)
                    got = got + base_ref[pl.ds(start, rows)].astype(F32)
                for which, row in targets:
                    out_refs[which][row : row + rows] = got.astype(out_refs[which].dtype)

    shapes = [jax.ShapeDtypeStruct((size, tokens), kind) for size, kind in outs]
    if not bare:
        shapes.append(jax.ShapeDtypeStruct((depth, tokens), LOW))
    return pl.pallas_call(
        body,
        in_specs=[SMEM, ANY] + [VMEM] * (count + (base is not None)),
        out_specs=[VMEM] * len(shapes),
        out_shape=shapes,
        scratch_shapes=[
            pltpu.VMEM((slots, rows, depth), LOW),
            pltpu.SemaphoreType.DMA((slots,)),
        ],
        compiler_params=params(),
        cost_estimate=pl.CostEstimate(
            flops=2 * tokens * rows * depth * steps,
            bytes_accessed=2 * rows * depth * steps,
            transcendentals=0,
        ),
    )(flags, mat, *sources, *([] if base is None else [base]))


def turned(right_ref, grad_ref):
    right_ref[...] = grad_ref[...].T.astype(LOW)


def hidden_of(right_ref, own_ref, other_ref, slope_ref):
    total = own_ref[...] + other_ref[...].astype(F32)
    right_ref[...] = (total * slope_ref[...]).astype(LOW)


def split_rows(flags, mat):
    rows, cols = mat.shape
    step = 256
    half = step // 2
    count = rows // step
    slots = 4

    def body(s, mat_ref, out_ref, buf, done, sem_in, sem_out):
        def fetch(i, slot):
            piece = mat_ref.at[pl.ds(pl.multiple_of(i * step, step), step)]
            return pltpu.make_async_copy(piece, buf.at[slot], sem_in.at[slot])

        def put(i, slot):
            piece = out_ref.at[:, pl.ds(pl.multiple_of(i * half, half), half)]
            return pltpu.make_async_copy(done.at[slot], piece, sem_out.at[slot])

        @pl.when(s[0] == 1)
        def _():
            to = lax.broadcasted_iota(jnp.int32, (step, step), 0)
            source = lax.broadcasted_iota(jnp.int32, (step, step), 1)
            wanted = jnp.where(to < half, 2 * to, 2 * (to - half) + 1)
            pick = jnp.where(source == wanted, 1.0, 0.0).astype(LOW)
            for i in range(slots):
                fetch(i, i).start()

            @pl.loop(0, count // slots)
            def _(turn):
                for slot in range(slots):
                    i = turn * slots + slot
                    fetch(i, slot).wait()

                    @pl.when(turn > 0)
                    def _():
                        put(i - slots, slot).wait()

                    got = jnp.dot(pick, buf[slot], preferred_element_type=F32).astype(LOW)
                    done[slot, 0] = got[:half]
                    done[slot, 1] = got[half:]

                    @pl.when(turn < count // slots - 1)
                    def _():
                        fetch(i + slots, slot).start()

                    put(i, slot).start()

            for slot in range(slots):
                put(count - slots + slot, slot).wait()

    out = pl.pallas_call(
        body,
        in_specs=[SMEM, ANY],
        out_specs=ANY,
        out_shape=jax.ShapeDtypeStruct((2, rows // 2, cols), LOW),
        scratch_shapes=[
            pltpu.VMEM((slots, step, cols), LOW),
            pltpu.VMEM((slots, 2, half, cols), LOW),
            pltpu.SemaphoreType.DMA((slots,)),
            pltpu.SemaphoreType.DMA((slots,)),
        ],
        compiler_params=params(),
        cost_estimate=pl.CostEstimate(
            flops=2 * rows * step * cols, bytes_accessed=4 * rows * cols, transcendentals=0
        ),
    )(flags, mat)
    return out.reshape(rows, cols)


def slope_of(flags, pre, start, tokens, half):
    cols = divisor(half, 768)
    per_half = half // cols

    def body(s, pre_ref, out_ref):
        out_ref[...] = gelu_slope(pre_ref[...]).T

    return pl.pallas_call(
        body,
        grid_spec=pltpu.PrefetchScalarGridSpec(
            num_scalar_prefetch=1,
            grid=(tokens // LANES, per_half),
            in_specs=[
                pl.BlockSpec((LANES, cols), lambda i, j, s: (start // LANES + i, s[1] * per_half + j))
            ],
            out_specs=pl.BlockSpec((cols, LANES), lambda i, j, s: (j, i)),
        ),
        out_shape=jax.ShapeDtypeStruct((half, tokens), F32),
        compiler_params=params(),
        cost_estimate=pl.CostEstimate(
            flops=40 * half * tokens, bytes_accessed=8 * half * tokens, transcendentals=0
        ),
    )(flags, pre)


def join(flags, grad, parts):
    tokens, columns = grad.shape
    width = columns // PARTS

    def body(s, grad_ref, *refs):
        part_refs, (low_ref, term_ref) = refs[:PARTS], refs[PARTS:]

        @pl.when(s[0] == 1)
        def _():
            for slot, ref in enumerate(part_refs):
                start = pl.multiple_of(lax.bitwise_xor(s[2], slot) * width, LANES)
                term = ref[...]
                term_ref[pl.ds(start, width)] = term
                total = grad_ref[:, pl.ds(start, width)].T + term.astype(F32)
                low_ref[pl.ds(start, width)] = total.astype(LOW)

    shape = jax.ShapeDtypeStruct((columns, tokens), LOW)
    return pl.pallas_call(
        body,
        in_specs=[SMEM] + [VMEM] * (1 + PARTS),
        out_specs=[VMEM, VMEM],
        out_shape=[shape, shape],
        compiler_params=params(),
        cost_estimate=pl.CostEstimate(
            flops=4 * columns * tokens, bytes_accessed=4 * columns * tokens, transcendentals=0
        ),
    )(flags, grad, *parts)


def finish(flags, out, grad, start, term, parts):
    columns, tokens = term.shape
    width = columns // PARTS
    total_tokens = grad.shape[0]

    def body(s, *refs):
        grad_ref, term_ref, *part_refs = refs[int(out is not None) : -2]
        out_ref, joined = refs[-2:]
        for slot, ref in enumerate(part_refs):
            start = pl.multiple_of(lax.bitwise_xor(s[2], slot) * width, LANES)
            joined[pl.ds(start, width)] = ref[...]

        @pl.when(s[0] == 0)
        def _():
            out_ref[...] = grad_ref[...] + joined[...].astype(F32).T

        @pl.when(s[0] == 1)
        def _():
            source = lax.broadcasted_iota(jnp.int32, (2 * LANES, 2 * LANES), 1)
            to = lax.broadcasted_iota(jnp.int32, (2 * LANES, 2 * LANES), 0)
            wanted = jnp.where(source < LANES, 2 * source, 2 * (source - LANES) + 1)
            pick = jnp.where(to == wanted, 1.0, 0.0).astype(LOW)
            for group in range(columns // (2 * LANES)):
                even_at = group * LANES
                odd_at = columns // 2 + group * LANES
                even = joined[even_at : even_at + LANES]
                odd = joined[odd_at : odd_at + LANES]
                pair = jnp.concatenate([even, odd], axis=0)
                woven = jnp.dot(pick, pair, preferred_element_type=F32)
                at = slice(group * 2 * LANES, (group + 1) * 2 * LANES)
                first = term_ref[at].astype(F32).T
                out_ref[:, at] = grad_ref[:, at] + first + woven.T

    earlier = [] if out is None else [out]
    piece = pl.BlockSpec((width, LANES), lambda i, s: (0, i))
    rows = pl.BlockSpec((LANES, columns), lambda i, s: (start // LANES + i, 0))
    return pl.pallas_call(
        body,
        grid_spec=pltpu.PrefetchScalarGridSpec(
            num_scalar_prefetch=1,
            grid=(tokens // LANES,),
            in_specs=[ANY] * len(earlier)
            + [rows, pl.BlockSpec((columns, LANES), lambda i, s: (0, i))]
            + [piece] * PARTS,
            out_specs=rows,
            scratch_shapes=[pltpu.VMEM((columns, LANES), LOW)],
        ),
        out_shape=jax.ShapeDtypeStruct((total_tokens, columns), F32),
        input_output_aliases={1: 0} if earlier else {},
        compiler_params=params(),
    )(flags, *earlier, grad, term, *parts)


def local(grad_out, weight_in, weight_out, pre_act):
    hids = lax.axis_size("hid")
    section = lax.axis_index("section")
    side = lax.axis_index("wid") % 2
    is_up = section == 1

    def scalars(active_section):
        active = (section == active_section).astype(jnp.int32)
        return jnp.stack([active, side, lax.axis_index("hid") % PARTS]).astype(jnp.int32)

    down, up = scalars(0), scalars(1)

    def within(active, distance, block, axis="wid"):
        size = lax.axis_size(axis)
        pairs = [(active * size + i, active * size + (i ^ distance)) for i in range(size)]
        return lax.ppermute(block, ("section", axis), pairs)

    def everywhere(distance, block, axis="hid"):
        size = lax.axis_size(axis)
        return lax.ppermute(block, axis, [(i, i ^ distance) for i in range(size)])

    mat_in = weight_in[0]
    mat_out = weight_out[0]
    quarter, hid_tile = mat_in.shape
    half = hid_tile // 2
    batches, batch_tokens, _ = grad_out.shape
    total = batches * batch_tokens
    unit = total // sum(SHARES)
    starts = [unit * sum(SHARES[:k]) for k in range(len(SHARES))]
    sizes = [unit * share for share in SHARES]
    chunks = range(len(SHARES))
    grad = grad_out.reshape(total, quarter)
    pre = pre_act[0].reshape(total, hid_tile)
    grads = [grad[starts[k] : starts[k] + sizes[k]] for k in chunks]

    split_out = split_rows(up, mat_out)

    hid_rows = divisor(half, 512)
    hid_steps = half // hid_rows
    part_rows = quarter // PARTS

    def in_order(*which):
        return lambda i, s, rows: ([(w, i * rows) for w in which], i * rows)

    def product_out(flags, mat, first_row, sources, prepare, tokens, kinds, base=None):
        return product(
            flags, mat, (hid_rows, quarter),
            lambda i, s: (first_row(s) + i * hid_rows, 0), hid_steps,
            sources, prepare, tokens, [(half, kind) for kind in kinds],
            functools.partial(in_order(*range(len(kinds))), rows=hid_rows), base,
        )

    def product_in(flags, place, sources, prepare, tokens, kind):
        return product(
            flags, mat_in, (part_rows, half), place, PARTS, sources, prepare, tokens,
            [(quarter, kind)], functools.partial(in_order(0), rows=part_rows),
        )

    def product_parts(flags, place, right, tokens, base):
        def part_of(i, s):
            return lax.bitwise_xor(s[2], (i + 1) % PARTS)

        return product(
            flags, mat_in, (part_rows, half), lambda i, s: place(part_of(i, s), s), PARTS,
            [right], None, tokens, [(part_rows, LOW)] * 3 + [(part_rows, F32)],
            lambda i, s: ([(i, 0)], part_of(i, s) * part_rows), base,
        )

    def scatter_hid(active, parts):
        *others, own = parts
        got = [within(active, d + 1, part, "hid") for d, part in enumerate(others)]
        for part in got:
            own = own + part.astype(F32)
        distance = PARTS
        while distance < hids:
            own = own + within(active, distance, own, "hid")
            distance *= 2
        return own.astype(LOW)

    def down_chunk(k, flags):
        tokens = sizes[k]
        sent, low = product_out(
            flags, mat_out, lambda s: (1 - s[1]) * half, [grads[k]], turned, tokens, (LOW,)
        )
        got = within(0, 1, sent)
        full, low_grad = product_out(
            flags, mat_out, lambda s: s[1] * half, [low], None, tokens, (F32, LOW), got
        )
        other = within(0, 2, low_grad)
        late, _ = lax.optimization_barrier((down, low_grad))
        slope = slope_of(late, pre, starts[k], tokens, half)
        hidden = ((full + other.astype(F32)) * slope).astype(LOW)
        swapped = within(0, 1, hidden)
        (partial,) = product_in(
            down, lambda i, s: (i * part_rows, s[1] * half), [hidden], None, tokens, F32
        )
        parts = product_parts(
            down, lambda i, s: (i * part_rows, (1 - s[1]) * half), swapped, tokens, partial
        )
        term = scatter_hid(0, parts)
        crossed = lax.ppermute(term, "section", [(0, 1)])
        gathered = [crossed] + [within(1, d, crossed, "hid") for d in range(1, PARTS)]
        return term, gathered, slope, low_grad

    def up_chunk(k, out, own_term, gathered, slope):
        tokens = sizes[k]
        low, term = join(up, grads[k], gathered)
        low_other = within(1, 1, low)
        (partial,) = product_out(
            up, split_out, lambda s: s[1] * half, [low], None, tokens, (F32,)
        )
        full, low_grad = product_out(
            up, split_out, lambda s: (1 - s[1]) * half, [low_other], None, tokens, (F32, LOW), partial
        )
        other = within(1, 2, low_grad)

        def place(part, core):
            row = core * (PARTS // 2) + part % (PARTS // 2)
            return row * part_rows, part // (PARTS // 2) * half

        sent, hidden = product_in(
            up, lambda i, s: place(i, 1 - s[1]), [full, other, slope], hidden_of, tokens, F32
        )
        got = within(1, 1, sent)
        parts = product_parts(up, lambda i, s: place(i, s[1]), hidden, tokens, got)
        last = jnp.where(is_up, scatter_hid(1, parts), own_term)
        parts = [last] + [everywhere(d, last) for d in range(1, PARTS)]
        return finish(up, out, grad, starts[k], term, parts)

    firsts = []
    flags = down
    for k in chunks:
        *first, low_grad = down_chunk(k, flags)
        firsts.append(first)
        flags, _ = lax.optimization_barrier((down, low_grad))
    out = None
    for k in chunks:
        out = up_chunk(k, out, *firsts[k])
    return out.reshape(1, batches, batch_tokens, quarter)


def solution(mesh):
    return jax.shard_map(
        local,
        mesh=mesh,
        in_specs=(
            P(None, None, "wid"),
            P("section", "wid", "hid"),
            P("section", "hid", "wid"),
            P("section", None, None, "hid"),
        ),
        out_specs=P("section", None, None, "wid"),
        check_vma=False,
    )
```

time: 443 us -> 506 us (1.14); the launches traced: 440 us -> 497 us
  blocking collectives: 117 us -> 0 us
  local copies, waits for them, and re-layouts: 31.6 us -> 107 us
  starting transfers between devices: 58.4 us -> 126 us
  waiting for transfers between devices: 64.8 us -> 124 us
  other arithmetic: 24.5 us -> 7.06 us
  Pallas kernels: 143 us -> 131 us
    all_gather x6 -> x0, blocking collectives: 117 us -> none  [gather_hid(): got = lax.all_gather(term, 'hid', axis=0)]
    ppermute x18 -> x54, starting transfers between devices: 29 us -> 122 us  [the longest x45 95.8 us: within(): return lax.ppermute(block, ('section', axis), pairs)]
    unnamed x50 -> x146, local copies, waits for them, and re-layouts: 20.3 us -> 105 us
    ppermute x3, waiting for transfers between devices: 42 us -> 113 us  [down_chunk(): crossed = lax.ppermute(term, 'section', [(0, 1)])]
    all_to_all x6 -> x0, starting transfers between devices: 25.5 us -> none  [reduce_hid(): got = lax.all_to_all(parts, 'hid', 0, 0)]
    all_to_all x6 -> x0, waiting for transfers between devices: 14.8 us -> none  [reduce_hid(): got = lax.all_to_all(parts, 'hid', 0, 0)]
    pallas_call x25 -> x31, Pallas kernels: 137 us -> 125 us  [the longest x24 102 us: product(): pl.pallas_call(body, in_specs=[SMEM, ANY] + [VMEM] * (count + (base is no...]
    dynamic_slice x2 -> x0, local copies, waits for them, and re-layouts: 7.76 us -> none  [slope_of(): own = lax.dynamic_slice(pre, (starts[k], side * half), (sizes[k], half))]
  transfers between devices with their start and end apart: 27 -> 57, of which waited for: 7 -> 9; matrix products, arithmetic and copies ran while one was open for 11% -> 1% of each run, Pallas kernels for 29% -> 25%
where the time goes in v3:
time: 506 us; the launch traced here: 497 us
  Pallas kernels  131 us (26%)
  starting transfers between devices  126 us (25%)
  waiting for transfers between devices  124 us (25%)
  local copies, waits for them, and re-layouts  107 us (21%)
  other arithmetic  7.06 us (1%)
    ppermute x3, waiting for transfers between devices, down_chunk(): crossed = lax.ppermute(term, 'section', [(0, 1)])  113 us
    unnamed x146, local copies, waits for them, and re-layouts  105 us
    pallas_call x24, Pallas kernels, product(): pl.pallas_call(body, in_specs=[SMEM, ANY] + [VMEM] * (count + (base is no...  102 us
    ppermute x45, starting transfers between devices, within(): return lax.ppermute(block, ('section', axis), pairs)  95.8 us
    ppermute x9, starting transfers between devices, everywhere(): return lax.ppermute(block, axis, [(i, i ^ distance) for i in range(size)])  26.6 us
    pallas_call x1, Pallas kernels, split_rows(): pl.pallas_call(body, in_specs=[SMEM, ANY], out_specs=ANY, out_shape=jax.S...  13.2 us
  transfers between devices with their start and end apart: 57, of which 9 were waited for; matrix products, arithmetic and copies ran while one was open for 1% of the time, Pallas kernels for 25%

profile of v3, /device:TPU:2, one launch (start us, length us, event | category | flops | bytes accessed | tf_op | source)
XLA Modules:
  0.0 497.5 jit_solution(2234470791361983301)
XLA Ops:
  1.6 6.8 %copy-done.4 = bf16[1,6144,1536]{2,1,0:T(8,128)(2,1)S(1)} copy-done((bf16[1,6144,1536]{2,1,0:T(8,128)(2,1)S(1)}, bf16[1,6144,1536]{2,1,0:T(8,128)(2,1)}, u32[]{:S(2)}) %copy-start.4) | copy-done | bytes 18874392
  38.7 6.4 %copy-done.5 = bf16[1,6144,1536]{2,1,0:T(8,128)(2,1)S(1)} copy-done((bf16[1,6144,1536]{2,1,0:T(8,128)(2,1)S(1)}, bf16[1,6144,1536]{2,1,0:T(8,128)(2,1)}, u32[]{:S(2)}) %copy-start.5) | copy-done | bytes 18874392
  49.0 104.1 %collective-permute-done.25.refs_0_ = bf16[384,256]{1,0:T(8,128)(2,1)} collective-permute-done((bf16[384,256]{1,0:T(8,128)(2,1)S(1)}, bf16[384,256]{1,0:T(8,128)(2,1)}, u32[]{:S(2)}, u32[]{:S(2)}) %collective-permute-start.25) | collective-permute-done | bytes 196640 | tf_op jit(solution)/shard_map/ppermute | solution.py:379
  163.2 13.2 %shard_map.52 = bf16[2,3072,1536]{2,1,0:T(8,128)(2,1)S(1)} custom-call(s32[3]{0:T(128)S(1)} %add_add_fusion.s, bf16[6144,1536]{1,0:T(8,128)(2,1)} %bitcast.22), custom_call_target="tpu_custom_call" | custom-call | flops 4831838208 | bytes 37748736 | tf_op jit(solution)/shard_map/pallas_call | solution.py:153
  176.5 6.4 %copy-done.7 = bf16[2,3072,1536]{2,1,0:T(8,128)(2,1)} copy-done((bf16[2,3072,1536]{2,1,0:T(8,128)(2,1)}, bf16[2,3072,1536]{2,1,0:T(8,128)(2,1)S(1)}, u32[]{:S(2)}) %copy-start.7) | copy-done | bytes 18874392
  190.0 6.4 %copy-done.6 = bf16[1,6144,1536]{2,1,0:T(8,128)(2,1)S(1)} copy-done((bf16[1,6144,1536]{2,1,0:T(8,128)(2,1)S(1)}, bf16[1,6144,1536]{2,1,0:T(8,128)(2,1)}, u32[]{:S(2)}) %copy-start.6) | copy-done | bytes 18874392
  209.6 6.9 %copy-done.8 = bf16[2,3072,1536]{2,1,0:T(8,128)(2,1)S(1)} copy-done((bf16[2,3072,1536]{2,1,0:T(8,128)(2,1)S(1)}, bf16[2,3072,1536]{2,1,0:T(8,128)(2,1)}, u32[]{:S(2)}) %copy-start.8) | copy-done | bytes 18874392
  216.5 7.1 %shard_map.64.refs_1_ = f32[3072,256]{1,0:T(8,128)S(1)} custom-call(s32[3]{0:T(128)S(1)} %add_add_fusion.s, bf16[6144,1536]{1,0:T(8,128)(2,1)S(1)} %bitcast.29, bf16[1536,256]{1,0:T(8,128)(2,1)S(1)} %get-tuple-element.91.refs_0_), custom_call_target="tpu_custom_call" | custom-call | flops 2415919104 | bytes 9437184 | tf_op jit(solution)/shard_map/pallas_call | solution.py:78
  223.6 8.7 %shard_map.65 = (f32[3072,256]{1,0:T(8,128)S(1)}, bf16[3072,256]{1,0:T(8,128)(2,1)}) custom-call(s32[3]{0:T(128)S(1)} %add_add_fusion.s, bf16[6144,1536]{1,0:T(8,128)(2,1)S(1)} %bitcast.30, bf16[1536,256]{1,0:T(8,128)(2,1)S(1)} %collective-permute-done.29.refs_0_, f32[3072,256]{1,0:T(8,128)S(1)} %shard_map.64.refs_1_), custom_call_target="tpu_custom_call" | custom-call | flops 2415919104 | bytes 9437184 | tf_op jit(solution)/shard_map/pallas_call | solution.py:78
  280.4 7.0 %shard_map.53.refs_1_ = f32[3072,128]{1,0:T(8,128)S(1)} custom-call(s32[3]{0:T(128)S(1)} %add_add_fusion.s, bf16[6144,1536]{1,0:T(8,128)(2,1)S(1)} %bitcast.31, bf16[1536,128]{1,0:T(8,128)(2,1)S(1)} %get-tuple-element.72.refs_0_), custom_call_target="tpu_custom_call" | custom-call | flops 1207959552 | bytes 9437184 | tf_op jit(solution)/shard_map/pallas_call | solution.py:78
  307.7 8.2 %shard_map.54 = (f32[3072,128]{1,0:T(8,128)S(1)}, bf16[3072,128]{1,0:T(8,128)(2,1)}) custom-call(s32[3]{0:T(128)S(1)} %add_add_fusion.s, bf16[6144,1536]{1,0:T(8,128)(2,1)S(1)} %bitcast.32, bf16[1536,128]{1,0:T(8,128)(2,1)S(1)} %collective-permute-done.10.refs_0_, f32[3072,128]{1,0:T(8,128)S(1)} %shard_map.53.refs_1_), custom_call_target="tpu_custom_call" | custom-call | flops 1207959552 | bytes 9437184 | tf_op jit(solution)/shard_map/pallas_call | solution.py:78
  330.6 9.1 %shard_map.66 = (f32[1536,256]{1,0:T(8,128)}, bf16[3072,256]{1,0:T(8,128)(2,1)S(1)}) custom-call(s32[3]{0:T(128)S(1)} %add_add_fusion.s, bf16[1536,6144]{1,0:T(8,128)(2,1)} %bitcast.10, f32[3072,256]{1,0:T(8,128)S(1)} %copy-done.31, bf16[3072,256]{1,0:T(8,128)(2,1)S(1)} %copy-done.33, f32[3072,256]{1,0:T(8,128)S(1)} %copy-done.16), custom_call_target="tpu_custom_call" | custom-call | flops 2415919104 | bytes 9437184 | tf_op jit(solution)/shard_map/pallas_call | solution.py:78
  342.2 7.0 %shard_map.75.refs_1_ = f32[3072,128]{1,0:T(8,128)S(1)} custom-call(s32[3]{0:T(128)S(1)} %add_add_fusion.s, bf16[6144,1536]{1,0:T(8,128)(2,1)S(1)} %bitcast.35, bf16[1536,128]{1,0:T(8,128)(2,1)S(1)} %get-tuple-element.110.refs_0_), custom_call_target="tpu_custom_call" | custom-call | flops 1207959552 | bytes 9437184 | tf_op jit(solution)/shard_map/pallas_call | solution.py:78
  351.3 6.4 %copy-done.11 = bf16[2,3072,1536]{2,1,0:T(8,128)(2,1)S(1)} copy-done((bf16[2,3072,1536]{2,1,0:T(8,128)(2,1)S(1)}, bf16[2,3072,1536]{2,1,0:T(8,128)(2,1)}, u32[]{:S(2)}) %copy-start.11) | copy-done | bytes 18874392
  360.0 7.3 %shard_map.76 = (f32[3072,128]{1,0:T(8,128)S(1)}, bf16[3072,128]{1,0:T(8,128)(2,1)S(1)}) custom-call(s32[3]{0:T(128)S(1)} %add_add_fusion.s, bf16[6144,1536]{1,0:T(8,128)(2,1)S(1)} %bitcast.36, bf16[1536,128]{1,0:T(8,128)(2,1)S(1)} %copy-done.53, f32[3072,128]{1,0:T(8,128)S(1)} %copy-done.28), custom_call_target="tpu_custom_call" | custom-call | flops 1207959552 | bytes 9437184 | tf_op jit(solution)/shard_map/pallas_call | solution.py:78
  376.2 8.1 %shard_map.55 = (f32[1536,128]{1,0:T(8,128)S(1)}, bf16[3072,128]{1,0:T(8,128)(2,1)S(1)}) custom-call(s32[3]{0:T(128)S(1)} %add_add_fusion.s, bf16[1536,6144]{1,0:T(8,128)(2,1)S(1)} %bitcast.17, f32[3072,128]{1,0:T(8,128)S(1)} %copy-done.37, bf16[3072,128]{1,0:T(8,128)(2,1)} %collective-permute-done.11.refs_1_, f32[3072,128]{1,0:T(8,128)S(1)} %copy-done.20), custom_call_target="tpu_custom_call" | custom-call | flops 1207959552 | bytes 9437184 | tf_op jit(solution)/shard_map/pallas_call | solution.py:78
  388.7 6.4 %copy-done.3 = bf16[1,1536,6144]{2,1,0:T(8,128)(2,1)S(1)} copy-done((bf16[1,1536,6144]{2,1,0:T(8,128)(2,1)S(1)}, bf16[1,1536,6144]{2,1,0:T(8,128)(2,1)}, u32[]{:S(2)}) %copy-start.3) | copy-done | bytes 18874392
  395.1 7.1 %shard_map.77 = (f32[1536,128]{1,0:T(8,128)S(1)}, bf16[3072,128]{1,0:T(8,128)(2,1)S(1)}) custom-call(s32[3]{0:T(128)S(1)} %add_add_fusion.s, bf16[1536,6144]{1,0:T(8,128)(2,1)S(1)} %bitcast.18, f32[3072,128]{1,0:T(8,128)S(1)} %get-tuple-element.111.refs_0_, bf16[3072,128]{1,0:T(8,128)(2,1)S(1)} %collective-permute-done.49.refs_1_, f32[3072,128]{1,0:T(8,128)S(1)} %copy-done.22), custom_call_target="tpu_custom_call" | custom-call | flops 1207959552 | bytes 9437184 | tf_op jit(solution)/shard_map/pallas_call | solution.py:78
  404.1 6.9 %shard_map.56 = (bf16[384,128]{1,0:T(8,128)(2,1)S(1)}, bf16[384,128]{1,0:T(8,128)(2,1)S(1)}, bf16[384,128]{1,0:T(8,128)(2,1)S(1)}, f32[384,128]{1,0:T(8,128)S(1)}) custom-call(s32[3]{0:T(128)S(1)} %add_add_fusion.s, bf16[1536,6144]{1,0:T(8,128)(2,1)S(1)} %bitcast.19, bf16[3072,128]{1,0:T(8,128)(2,1)S(1)} %get-tuple-element.75.refs_0_, ...), custom_call_target="tpu_custom_call" | custom-call | flops 1207959552 | bytes 9437184 | tf_op jit(solution)/shard_map/pallas_call | solution.py:78
  421.2 7.9 %shard_map.67 = (bf16[384,256]{1,0:T(8,128)(2,1)S(1)}, bf16[384,256]{1,0:T(8,128)(2,1)S(1)}, bf16[384,256]{1,0:T(8,128)(2,1)S(1)}, f32[384,256]{1,0:T(8,128)S(1)}) custom-call(s32[3]{0:T(128)S(1)} %add_add_fusion.s, bf16[1536,6144]{1,0:T(8,128)(2,1)S(1)} %bitcast.20, bf16[3072,256]{1,0:T(8,128)(2,1)S(1)} %copy-done.35, ...), custom_call_target="tpu_custom_call" | custom-call | flops 2415919104 | bytes 9437184 | tf_op jit(solution)/shard_map/pallas_call | solution.py:78
  441.1 6.9 %shard_map.78 = (bf16[384,128]{1,0:T(8,128)(2,1)S(1)}, bf16[384,128]{1,0:T(8,128)(2,1)S(1)}, bf16[384,128]{1,0:T(8,128)(2,1)S(1)}, f32[384,128]{1,0:T(8,128)S(1)}) custom-call(s32[3]{0:T(128)S(1)} %add_add_fusion.s, bf16[1536,6144]{1,0:T(8,128)(2,1)S(1)} %bitcast.21, bf16[3072,128]{1,0:T(8,128)(2,1)S(1)} %get-tuple-element.113.refs_0_, ...), custom_call_target="tpu_custom_call" | custom-call | flops 1207959552 | bytes 9437184 | tf_op jit(solution)/shard_map/pallas_call | solution.py:78
  459.7 7.8 %collective-permute-start.16 = (bf16[384,128]{1,0:T(8,128)(2,1)S(1)}, bf16[384,128]{1,0:T(8,128)(2,1)S(1)}, u32[]{:S(2)}, u32[]{:S(2)}) collective-permute-start(bf16[384,128]{1,0:T(8,128)(2,1)S(1)} %fusion.1.refs_2_), channel_id=1, source_target_pairs={{0,4},{4,0},{8,12},{12,8},{1,5},{5,1},{9,13},{13,9},{2,6},{6,2},{1... | collective-permute-start | bytes 294920 | tf_op jit(solution)/shard_map/ppermute | solution.py:298
  471.1 7.5 %collective-permute-start.35 = (bf16[384,256]{1,0:T(8,128)(2,1)S(1)}, bf16[384,256]{1,0:T(8,128)(2,1)S(1)}, u32[]{:S(2)}, u32[]{:S(2)}) collective-permute-start(bf16[384,256]{1,0:T(8,128)(2,1)S(1)} %fusion.refs_3_), channel_id=1, source_target_pairs={{0,4},{4,0},{8,12},{12,8},{1,5},{5,1},{9,13},{13,9},{2,6},{6,2},{1... | collective-permute-start | bytes 589832 | tf_op jit(solution)/shard_map/ppermute | solution.py:298
  480.2 8.3 %collective-permute-start.54 = (bf16[384,128]{1,0:T(8,128)(2,1)S(1)}, bf16[384,128]{1,0:T(8,128)(2,1)S(1)}, u32[]{:S(2)}, u32[]{:S(2)}) collective-permute-start(bf16[384,128]{1,0:T(8,128)(2,1)S(1)} %fusion.2.refs_3_), channel_id=1, source_target_pairs={{0,4},{4,0},{8,12},{12,8},{1,5},{5,1},{9,13},{13,9},{2,6},{6,2},{1... | collective-permute-start | bytes 294920 | tf_op jit(solution)/shard_map/ppermute | solution.py:298
  (286 shorter events, 217.5 us)
Async XLA Ops:
  37.2 168.6 %collective-permute-start.1 = (bf16[3072,128]{1,0:T(8,128)(2,1)}, bf16[3072,128]{1,0:T(8,128)(2,1)}, u32[]{:S(2)}, u32[]{:S(2)}) collective-permute-start(bf16[3072,128]{1,0:T(8,128)(2,1)} %get-tuple-element.65), channel_id=1, source_target_pairs={{0,2},{1,3},{2,0},{3,1},{4,6},{5,7},{6,4},{7,5},{8,10},{9,11},{10,... | collective-permute-start | bytes 2359304 | tf_op jit(solution)/shard_map/ppermute | solution.py:294
  46.7 142.4 %collective-permute-start.38 = (bf16[3072,128]{1,0:T(8,128)(2,1)}, bf16[3072,128]{1,0:T(8,128)(2,1)S(1)}, u32[]{:S(2)}, u32[]{:S(2)}) collective-permute-start(bf16[3072,128]{1,0:T(8,128)(2,1)} %get-tuple-element.101), channel_id=1, source_target_pairs={{0,1},{1,0},{2,3},{3,2},{4,5},{5,4},{6,7},{7,6},{8,9},{9,8},{10,11... | collective-permute-start | bytes 2359304 | tf_op jit(solution)/shard_map/ppermute | solution.py:294
  47.6 105.5 %collective-permute-start.25 = (bf16[384,256]{1,0:T(8,128)(2,1)S(1)}, bf16[384,256]{1,0:T(8,128)(2,1)}, u32[]{:S(2)}, u32[]{:S(2)}) collective-permute-start(bf16[384,256]{1,0:T(8,128)(2,1)S(1)} %add_convert_fusion.1), channel_id=1, source_target_pairs={{0,16},{1,17},{2,18},{3,19},{4,20},{5,21},{6,22},{7,23},{8,24},{9,... | collective-permute-start | bytes 589832 | tf_op jit(solution)/shard_map/ppermute | solution.py:379
  153.1 47.7 %collective-permute-start.28 = (bf16[384,256]{1,0:T(8,128)(2,1)}, bf16[384,256]{1,0:T(8,128)(2,1)S(1)}, u32[]{:S(2)}, u32[]{:S(2)}) collective-permute-start(bf16[384,256]{1,0:T(8,128)(2,1)} %collective-permute-done.25.refs_0_), channel_id=1, source_target_pairs={{16,28},{20,24},{24,20},{28,16},{17,29},{21,25},{25,21},{29,17},{1... | collective-permute-start | bytes 589832 | tf_op jit(solution)/shard_map/ppermute | solution.py:294
  158.6 42.2 %collective-permute-start.27 = (bf16[384,256]{1,0:T(8,128)(2,1)}, bf16[384,256]{1,0:T(8,128)(2,1)S(1)}, u32[]{:S(2)}, u32[]{:S(2)}) collective-permute-start(bf16[384,256]{1,0:T(8,128)(2,1)} %collective-permute-done.25.refs_0_), channel_id=1, source_target_pairs={{16,24},{20,28},{24,16},{28,20},{17,25},{21,29},{25,17},{29,21},{1... | collective-permute-start | bytes 589832 | tf_op jit(solution)/shard_map/ppermute | solution.py:294
  160.5 40.2 %collective-permute-start.26 = (bf16[384,256]{1,0:T(8,128)(2,1)}, bf16[384,256]{1,0:T(8,128)(2,1)S(1)}, u32[]{:S(2)}, u32[]{:S(2)}) collective-permute-start(bf16[384,256]{1,0:T(8,128)(2,1)} %collective-permute-done.25.refs_0_), channel_id=1, source_target_pairs={{16,20},{20,16},{24,28},{28,24},{17,21},{21,17},{25,29},{29,25},{1... | collective-permute-start | bytes 589832 | tf_op jit(solution)/shard_map/ppermute | solution.py:294
  199.1 37.1 %collective-permute-start.39 = (bf16[3072,128]{1,0:T(8,128)(2,1)}, bf16[3072,128]{1,0:T(8,128)(2,1)}, u32[]{:S(2)}, u32[]{:S(2)}) collective-permute-start(bf16[3072,128]{1,0:T(8,128)(2,1)} %get-tuple-element.103), channel_id=1, source_target_pairs={{0,2},{1,3},{2,0},{3,1},{4,6},{5,7},{6,4},{7,5},{8,10},{9,11},{10,... | collective-permute-start | bytes 2359304 | tf_op jit(solution)/shard_map/ppermute | solution.py:294
  207.2 38.1 %collective-permute-start.2 = (bf16[3072,128]{1,0:T(8,128)(2,1)S(1)}, bf16[3072,128]{1,0:T(8,128)(2,1)S(1)}, u32[]{:S(2)}, u32[]{:S(2)}) collective-permute-start(bf16[3072,128]{1,0:T(8,128)(2,1)S(1)} %multiply_convert_fusion.2.refs_0_), channel_id=1, source_target_pairs={{0,1},{1,0},{2,3},{3,2},{4,5},{5,4},{6,7},{7,6},{8,9},{9,8},{10,11... | collective-permute-start | bytes 2359304 | tf_op jit(solution)/shard_map/ppermute | solution.py:294
  234.0 90.2 %collective-permute-start.30 = (bf16[3072,256]{1,0:T(8,128)(2,1)}, bf16[3072,256]{1,0:T(8,128)(2,1)S(1)}, u32[]{:S(2)}, u32[]{:S(2)}) collective-permute-start(bf16[3072,256]{1,0:T(8,128)(2,1)} %get-tuple-element.93), channel_id=1, source_target_pairs={{16,18},{17,19},{18,16},{19,17},{20,22},{21,23},{22,20},{23,21},{2... | collective-permute-start | bytes 4718600 | tf_op jit(solution)/shard_map/ppermute | solution.py:294
  237.6 28.4 %collective-permute-start.40 = (bf16[3072,128]{1,0:T(8,128)(2,1)S(1)}, bf16[3072,128]{1,0:T(8,128)(2,1)S(1)}, u32[]{:S(2)}, u32[]{:S(2)}) collective-permute-start(bf16[3072,128]{1,0:T(8,128)(2,1)S(1)} %multiply_convert_fusion.1.refs_0_), channel_id=1, source_target_pairs={{0,1},{1,0},{2,3},{3,2},{4,5},{5,4},{6,7},{7,6},{8,9},{9,8},{10,11... | collective-permute-start | bytes 2359304 | tf_op jit(solution)/shard_map/ppermute | solution.py:294
  270.6 30.6 %collective-permute-start.10 = (bf16[1536,128]{1,0:T(8,128)(2,1)S(1)}, bf16[1536,128]{1,0:T(8,128)(2,1)S(1)}, u32[]{:S(2)}, u32[]{:S(2)}) collective-permute-start(bf16[1536,128]{1,0:T(8,128)(2,1)S(1)} %get-tuple-element.72.refs_0_), channel_id=1, source_target_pairs={{16,17},{17,16},{18,19},{19,18},{20,21},{21,20},{22,23},{23,22},{2... | collective-permute-start | bytes 1179656 | tf_op jit(solution)/shard_map/ppermute | solution.py:294
  291.1 29.3 %collective-permute-start.47 = (bf16[384,128]{1,0:T(8,128)(2,1)S(1)}, bf16[384,128]{1,0:T(8,128)(2,1)S(1)}, u32[]{:S(2)}, u32[]{:S(2)}) collective-permute-start(bf16[384,128]{1,0:T(8,128)(2,1)S(1)} %collective-permute-done.44.refs_0_), channel_id=1, source_target_pairs={{16,28},{20,24},{24,20},{28,16},{17,29},{21,25},{25,21},{29,17},{1... | collective-permute-start | bytes 294920 | tf_op jit(solution)/shard_map/ppermute | solution.py:294
  294.5 26.0 %collective-permute-start.46 = (bf16[384,128]{1,0:T(8,128)(2,1)S(1)}, bf16[384,128]{1,0:T(8,128)(2,1)S(1)}, u32[]{:S(2)}, u32[]{:S(2)}) collective-permute-start(bf16[384,128]{1,0:T(8,128)(2,1)S(1)} %collective-permute-done.44.refs_0_), channel_id=1, source_target_pairs={{16,24},{20,28},{24,16},{28,20},{17,25},{21,29},{25,17},{29,21},{1... | collective-permute-start | bytes 294920 | tf_op jit(solution)/shard_map/ppermute | solution.py:294
  296.6 23.9 %collective-permute-start.45 = (bf16[384,128]{1,0:T(8,128)(2,1)S(1)}, bf16[384,128]{1,0:T(8,128)(2,1)S(1)}, u32[]{:S(2)}, u32[]{:S(2)}) collective-permute-start(bf16[384,128]{1,0:T(8,128)(2,1)S(1)} %collective-permute-done.44.refs_0_), channel_id=1, source_target_pairs={{16,20},{20,16},{24,28},{28,24},{17,21},{21,17},{25,29},{29,25},{1... | collective-permute-start | bytes 294920 | tf_op jit(solution)/shard_map/ppermute | solution.py:294
  317.0 52.7 %collective-permute-start.11 = (bf16[3072,128]{1,0:T(8,128)(2,1)}, bf16[3072,128]{1,0:T(8,128)(2,1)}, u32[]{:S(2)}, u32[]{:S(2)}) collective-permute-start(bf16[3072,128]{1,0:T(8,128)(2,1)} %get-tuple-element.74), channel_id=1, source_target_pairs={{16,18},{17,19},{18,16},{19,17},{20,22},{21,23},{22,20},{23,21},{2... | collective-permute-start | bytes 2359304 | tf_op jit(solution)/shard_map/ppermute | solution.py:294
  322.3 28.2 %collective-permute-start.48 = (bf16[1536,128]{1,0:T(8,128)(2,1)S(1)}, bf16[1536,128]{1,0:T(8,128)(2,1)S(1)}, u32[]{:S(2)}, u32[]{:S(2)}) collective-permute-start(bf16[1536,128]{1,0:T(8,128)(2,1)S(1)} %get-tuple-element.110.refs_0_), channel_id=1, source_target_pairs={{16,17},{17,16},{18,19},{19,18},{20,21},{21,20},{22,23},{23,22},{2... | collective-permute-start | bytes 1179656 | tf_op jit(solution)/shard_map/ppermute | solution.py:294
  339.7 81.5 %collective-permute-start.31 = (f32[1536,256]{1,0:T(8,128)}, f32[1536,256]{1,0:T(8,128)}, u32[]{:S(2)}, u32[]{:S(2)}) collective-permute-start(f32[1536,256]{1,0:T(8,128)} %get-tuple-element.95), channel_id=1, source_target_pairs={{16,17},{17,16},{18,19},{19,18},{20,21},{21,20},{22,23},{23,22},{2... | collective-permute-start | bytes 4718600 | tf_op jit(solution)/shard_map/ppermute | solution.py:294
  367.4 21.4 %collective-permute-start.49 = (bf16[3072,128]{1,0:T(8,128)(2,1)S(1)}, bf16[3072,128]{1,0:T(8,128)(2,1)S(1)}, u32[]{:S(2)}, u32[]{:S(2)}) collective-permute-start(bf16[3072,128]{1,0:T(8,128)(2,1)S(1)} %get-tuple-element.112), channel_id=1, source_target_pairs={{16,18},{17,19},{18,16},{19,17},{20,22},{21,23},{22,20},{23,21},{2... | collective-permute-start | bytes 2359304 | tf_op jit(solution)/shard_map/ppermute | solution.py:294
  402.2 38.9 %collective-permute-start.50 = (f32[1536,128]{1,0:T(8,128)S(1)}, f32[1536,128]{1,0:T(8,128)S(1)}, u32[]{:S(2)}, u32[]{:S(2)}) collective-permute-start(f32[1536,128]{1,0:T(8,128)S(1)} %get-tuple-element.114), channel_id=1, source_target_pairs={{16,17},{17,16},{18,19},{19,18},{20,21},{21,20},{22,23},{23,22},{2... | collective-permute-start | bytes 2359304 | tf_op jit(solution)/shard_map/ppermute | solution.py:294
  413.0 21.9 %collective-permute-start.14 = (bf16[384,128]{1,0:T(8,128)(2,1)S(1)}, bf16[384,128]{1,0:T(8,128)(2,1)S(1)}, u32[]{:S(2)}, u32[]{:S(2)}) collective-permute-start(bf16[384,128]{1,0:T(8,128)(2,1)S(1)} %get-tuple-element.79), channel_id=1, source_target_pairs={{16,24},{20,28},{24,16},{28,20},{17,25},{21,29},{25,17},{29,21},{1... | collective-permute-start | bytes 294920 | tf_op jit(solution)/shard_map/ppermute | solution.py:294
  416.9 22.6 %collective-permute-start.15 = (bf16[384,128]{1,0:T(8,128)(2,1)S(1)}, bf16[384,128]{1,0:T(8,128)(2,1)S(1)}, u32[]{:S(2)}, u32[]{:S(2)}) collective-permute-start(bf16[384,128]{1,0:T(8,128)(2,1)S(1)} %get-tuple-element.80), channel_id=1, source_target_pairs={{16,28},{20,24},{24,20},{28,16},{17,29},{21,25},{25,21},{29,17},{1... | collective-permute-start | bytes 294920 | tf_op jit(solution)/shard_map/ppermute | solution.py:294
  431.0 23.2 %collective-permute-start.33 = (bf16[384,256]{1,0:T(8,128)(2,1)S(1)}, bf16[384,256]{1,0:T(8,128)(2,1)S(1)}, u32[]{:S(2)}, u32[]{:S(2)}) collective-permute-start(bf16[384,256]{1,0:T(8,128)(2,1)S(1)} %get-tuple-element.98), channel_id=1, source_target_pairs={{16,24},{20,28},{24,16},{28,20},{17,25},{21,29},{25,17},{29,21},{1... | collective-permute-start | bytes 589832 | tf_op jit(solution)/shard_map/ppermute | solution.py:294
  434.9 21.2 %collective-permute-start.34 = (bf16[384,256]{1,0:T(8,128)(2,1)S(1)}, bf16[384,256]{1,0:T(8,128)(2,1)S(1)}, u32[]{:S(2)}, u32[]{:S(2)}) collective-permute-start(bf16[384,256]{1,0:T(8,128)(2,1)S(1)} %get-tuple-element.99), channel_id=1, source_target_pairs={{16,28},{20,24},{24,20},{28,16},{17,29},{21,25},{25,21},{29,17},{1... | collective-permute-start | bytes 589832 | tf_op jit(solution)/shard_map/ppermute | solution.py:294
  441.1 37.6 %collective-permute-start.17 = (bf16[384,128]{1,0:T(8,128)(2,1)S(1)}, bf16[384,128]{1,0:T(8,128)(2,1)S(1)}, u32[]{:S(2)}, u32[]{:S(2)}) collective-permute-start(bf16[384,128]{1,0:T(8,128)(2,1)S(1)} %fusion.1.refs_2_), channel_id=1, source_target_pairs={{0,8},{4,12},{8,0},{12,4},{1,9},{5,13},{9,1},{13,5},{2,10},{6,14},... | collective-permute-start | bytes 294920 | tf_op jit(solution)/shard_map/ppermute | solution.py:298
  (106 other events, 1293.0 us)
